TPU v7x, 256 devices: a whole 4x4x8 slice. The times are simulated.
256 devices in a mesh: fsdp: 64 (over x, z, core), dp: 4 (over y).
Axes of the slice: x: 4, y: 4, z: 8, core: 2. Of those that a mesh axis runs over, the one named last changes fastest.
Arguments:
- grad_parts: bfloat16 [4, 48, 1024, 1024], P('dp', None, 'fsdp')
- block_owner: int32 [48], replicated, may hold values from 0 to 63, as said below
- left_stat: float32 [64, 1024, 1024], P('fsdp', 'dp')
- right_stat: float32 [64, 1024, 1024], P('fsdp', 'dp')
- root_left: float32 [64, 1024, 1024], P('fsdp', 'dp'), as said below
- root_right: float32 [64, 1024, 1024], P('fsdp', 'dp'), as said below
Outputs:
- left_updated: float32 [64, 1024, 1024], P('fsdp', 'dp')
- right_updated: float32 [64, 1024, 1024], P('fsdp', 'dp')
- direction: float32 [48, 1024, 1024], P(None, 'fsdp', 'dp')
Inputs may be any that keep to these rules, and one draw needn't show every extreme that they name: `block_owner`: no two blocks share an owner; owners 0 and 63 always own a block. `root_right`: each slot is symmetric. `root_left`: each slot is symmetric.
All inputs are finite; a program needn't handle non-finite values.
Results may differ from a plain program's by a relative error of at most 0.0003.
Values may be sent and summed in bfloat16 or wider, within the bound.
No kernel may reach another device: no remote copies, remote signals or barrier semaphores. Data moves between devices by JAX's collectives and lax.ppermute only.
A program may use at most 64 MiB of HBM per device.

v0:
```python
import functools
import math

import jax
import jax.numpy as jnp
from jax import lax
from jax.experimental import pallas as pl
from jax.experimental.pallas import tpu as pltpu
from jax.sharding import PartitionSpec as P

AVERAGING = 0.9
GRAFT_EPS = 1e-06
VMEM_LIMIT = 24 * 1024 * 1024
STEPS = 1344
LARGEST = 252 * 128 + 127
FINE = 120.0

VMEM = pl.BlockSpec(memory_space=pltpu.VMEM)
SMEM = pl.BlockSpec(memory_space=pltpu.SMEM)
F32, BF16 = jnp.float32, jnp.bfloat16


def split(value):
    high = value.astype(BF16)
    low = (value - high.astype(F32)).astype(BF16)
    return high, low


def shrink(value):
    half = value.shape[1] // 2
    high = value.astype(BF16)
    wide = high.astype(F32)
    inverse = pl.reciprocal(jnp.where(wide == 0.0, 1.0, wide), approx=True)
    ratio = jnp.where(wide == 0.0, 0.0, (value - wide) * inverse)
    fine = jnp.clip(jnp.floor(ratio * (256.0 * FINE) + 0.5), -FINE, FINE)
    first, second = fine[:, :half], fine[:, half:]
    root = jnp.exp2(second * 0.5)
    word = (1.0 + jnp.abs(first) * (1.0 / 128.0)) * root * root
    return high, jnp.where(first < 0.0, -word, word).astype(BF16)


def widen(high, word):
    word = word.astype(F32)
    size = jnp.abs(word)
    second = jnp.floor(jnp.log(jnp.maximum(size, 1e-37)) * (1.0 / math.log(2.0)) + 0.01)
    root = jnp.exp2(second * -0.5)
    first = (size * root * root - 1.0) * 128.0
    first = jnp.where(word < 0.0, -first, first)
    fine = jnp.concatenate([first, second], axis=1) * (1.0 / (256.0 * FINE))
    return (high.astype(F32) * fine).astype(BF16)


def halves_kernel(whole_ref, top_ref, bottom_ref):
    half = top_ref.shape[0]
    top_ref[...] = whole_ref[:half, :]
    bottom_ref[...] = whole_ref[half:, :]


def widen_kernel(part_ref, out_ref):
    size = out_ref.shape[1] // 2
    high = part_ref[:, :size]
    out_ref[:, :size] = high
    out_ref[:, size:] = widen(high, part_ref[:, size:])


def dot3(left, right, left_dim, right_dim):
    dims = (((left_dim,), (right_dim,)), ((), ()))

    def one(a, b):
        return lax.dot_general(a, b, dims, preferred_element_type=F32)

    return one(left[0], right[0]) + (one(left[0], right[1]) + one(left[1], right[0]))


def like(shape, dtype=F32):
    return jax.ShapeDtypeStruct(shape, dtype)


def call(kernel, outs, operands, n_smem=0, smem_outs=(), flops=0, cost=4 << 20):
    several = isinstance(outs, tuple)
    out_specs = tuple(
        SMEM if i in smem_outs else VMEM for i in range(len(outs) if several else 1)
    )
    return pl.pallas_call(
        kernel,
        out_shape=outs,
        in_specs=[SMEM] * n_smem + [VMEM] * (len(operands) - n_smem),
        out_specs=out_specs if several else out_specs[0],
        compiler_params=pltpu.CompilerParams(vmem_limit_bytes=VMEM_LIMIT),
        cost_estimate=pl.CostEstimate(flops=flops, bytes_accessed=cost, transcendentals=0),
    )(*operands)


def around(index, size, parts):
    return pl.ds(pl.multiple_of(lax.rem(index, parts) * size, size), size)


def pack_kernel(place_ref, grad_ref, *out_refs):
    part = out_refs[0].shape[2]
    parts = len(out_refs)
    for k, out_ref in enumerate(out_refs):
        out_ref[...] = grad_ref[:, :, around(place_ref[0] + k, part, parts)]


def sum_kernel(owner_ref, *refs):
    *replica_refs, out_ref = refs
    part = replica_refs[0].shape[2]
    out_ref[...] = jnp.zeros_like(out_ref)

    @pl.loop(0, replica_refs[0].shape[0], unroll=8)
    def _(b):
        total = replica_refs[0][b].astype(F32)
        for ref in replica_refs[1:]:
            total = total + ref[b].astype(F32)
        owner = owner_ref[b]
        out_ref[owner, :, :part], out_ref[owner, :, part:] = shrink(total)


def root_pack_kernel(place_ref, root_ref, next_ref, previous_ref):
    size = root_ref.shape[0]
    parts = root_ref.shape[1] // size
    me = place_ref[0]

    def put(ref, slot, shift):
        high, word = shrink(root_ref[:, around(me + shift, size, parts)])
        ref[slot, :, :size] = high
        ref[slot, :, size:] = word

    for slot in range(3):
        put(next_ref, slot, slot)
    put(previous_ref, 0, 0)
    put(previous_ref, 1, parts - 1)


def root_join_kernel(place_ref, root_ref, after_ref, before_ref, far_ref, high_ref, low_ref):
    size = root_ref.shape[0]
    parts = root_ref.shape[1] // size
    me = place_ref[0]

    def put(i, j, value):
        rows, columns = around(me + i, size, parts), around(me + j, size, parts)
        for ref, half in zip((high_ref, low_ref), value):
            ref[rows, columns] = half
            if i != j:
                ref[columns, rows] = half.astype(F32).T.astype(BF16)

    def block(ref, slot):
        high = ref[slot, :, :size]
        return high, widen(high, ref[slot, :, size:])

    for j in range(parts):
        put(0, j, split(root_ref[:, around(me + j, size, parts)]))
    put(1, 1, block(after_ref, 0))
    put(1, 2, block(after_ref, 1))
    put(1, 3, block(after_ref, 2))
    put(3, 3, block(before_ref, 0))
    put(3, 2, block(before_ref, 1))
    put(2, 2, block(far_ref, 0))


def own_half(refs, me, part):
    rows = pl.ds(pl.multiple_of(lax.rem(me, 2) * part, part), part)
    top, bottom = refs[0][rows, :], refs[1][rows, :]
    return jnp.where(me < 2, top, bottom)


def pair(value):
    part = value.shape[1] // 2
    return value[:, :part], value[:, part:]


def statistics_kernel(scale, shifts, first, place_ref, *refs):
    count = 2 * len(shifts)
    own, parts = refs[:2], refs[2 : 2 + count]
    left_in, right_in, left_out, right_out = refs[2 + count :]
    me = place_ref[0]
    part, order = left_in.shape
    half = order // 2
    keep = AVERAGING if first else 1.0
    right_out[...] = right_in[...] * keep
    left = left_in[...] * keep
    sums = [left[:, :half], left[:, half:]]
    for i, shift in enumerate(shifts):
        blocks = parts[2 * i : 2 * i + 2]
        mine = pair(own_half(blocks, me, part))
        halves = [pair(ref[...]) for ref in blocks]
        for h in range(2):
            sums[h] = sums[h] + scale * dot3(mine, halves[h], 1, 1)
        term = dot3(pair(own[0][...]), halves[0], 0, 0) + dot3(pair(own[1][...]), halves[1], 0, 0)
        columns = around(me + shift, part, order // part)
        right_out[:, columns] += scale * term
    left_out[:, :half] = sums[0]
    left_out[:, half:] = sums[1]


def value_terms(me, shifts, parts, root_ref):
    part, order = root_ref.shape
    sums = [None, None]
    for i, shift in enumerate(shifts):
        root = split(root_ref[:, around(me + shift, part, order // part)])
        for h in range(2):
            term = dot3(parts[2 * i + h], root, 1, 1)
            sums[h] = term if sums[h] is None else sums[h] + term
    return sums


def value_kernel(shifts, first, place_ref, *refs):
    count = 2 * len(shifts)
    parts, root_ref = refs[:count], refs[count]
    *value_in, value_out = refs[count + 1 :]
    half = value_out.shape[0] // 2
    sums = value_terms(place_ref[0], shifts, [pair(ref[...]) for ref in parts], root_ref)
    for h in range(2):
        rows = slice(h * half, (h + 1) * half)
        value_out[rows, :] = sums[h] if first else sums[h] + value_in[0][rows, :]


def square_kernel(top_ref, bottom_ref, out_ref):
    total = jnp.zeros((), F32)
    for ref in (top_ref, bottom_ref):
        high, low = pair(ref[...])
        whole = high.astype(F32) + low.astype(F32)
        total = total + jnp.sum(whole * whole)
    out_ref[...] = jnp.full(out_ref.shape, total)


def result_kernel(
    shift, place_ref, top_ref, bottom_ref, root_ref, value_ref, high_ref, low_ref, own_square, out_ref, square_ref, peak_ref
):
    order, part = value_ref.shape
    half = order // 2
    coded = [(ref[:, :part], ref[:, part:]) for ref in (top_ref, bottom_ref)]
    pieces = [(high, widen(high, word)) for high, word in coded]
    sums = value_terms(place_ref[0], (shift,), pieces, root_ref)
    halves = [split(sums[h] + value_ref[h * half : (h + 1) * half, :]) for h in range(2)]
    value = [jnp.concatenate([halves[0][i], halves[1][i]], axis=0) for i in range(2)]
    total = jnp.zeros((), F32)
    peak = jnp.zeros((), F32)
    for i in range(2):
        rows = slice(i * half, (i + 1) * half)
        block = dot3((high_ref[rows, :], low_ref[rows, :]), value, 1, 0)
        out_ref[rows, :] = block
        total = total + jnp.sum(block * block)
        peak = jnp.maximum(peak, jnp.max(jnp.abs(block)))
    first = lax.broadcasted_iota(jnp.int32, square_ref.shape, 1) == 0
    square_ref[...] = jnp.where(first, own_square[...], total)
    peak_ref[...] = jnp.full(peak_ref.shape, peak)


def encode(ratio):
    size = jnp.abs(ratio)
    code = jnp.floor(jnp.log(jnp.maximum(size, 1e-30)) * (STEPS / math.log(2.0)) + (LARGEST + 0.5))
    code = jnp.minimum(code, float(LARGEST))
    exponent = jnp.floor(code * (1.0 / 128.0))
    root = jnp.exp2((exponent - 126.0) * 0.5)
    number = (1.0 + (code - exponent * 128.0) * (1.0 / 128.0)) * root * root
    number = jnp.where(code < 128.0, 0.0, number)
    return jnp.where(ratio < 0.0, -number, number).astype(BF16)


def decode(number):
    number = number.astype(F32)
    size = jnp.abs(number)
    exponent = jnp.floor(jnp.log(jnp.maximum(size, 2e-38)) * (1.0 / math.log(2.0)) + 0.002)
    root = jnp.exp2(exponent * -0.5)
    code = 128.0 * (exponent + 125.0 + size * root * root)
    value = jnp.exp2((code - LARGEST) * (1.0 / STEPS))
    value = jnp.where(size == 0.0, 0.0, value)
    return jnp.where(number < 0.0, -value, value)


def encode_kernel(value_ref, peak_ref, out_ref):
    slab = value_ref.shape[0] // out_ref.shape[0]
    lanes = out_ref.shape[2]
    peak = jnp.max(peak_ref[...])
    inverse = jnp.where(peak > 1e-37, 1.0 / jnp.maximum(peak, 1e-37), 0.0)
    pieces = value_ref.shape[1] // lanes

    @pl.loop(0, out_ref.shape[0], unroll=16)
    def _(o):
        rows = pl.ds(pl.multiple_of(o * slab, slab), slab)
        for i in range(pieces):
            value = value_ref[rows, i * lanes : (i + 1) * lanes]
            out_ref[o, i * slab : (i + 1) * slab, :] = encode(value * inverse)


def stamp_kernel(peak_ref, *refs):
    *square_refs, codes_ref, out_ref = refs
    total = square_refs[0][...]
    for ref in square_refs[1:]:
        total = total + ref[...]
    count, rows, lanes = out_ref.shape
    gradient, result = total[:, :1], total[:, 1:2]
    scale = peak_ref[...] * (jnp.sqrt(gradient) * lax.rsqrt(result + GRAFT_EPS))
    row = lax.broadcasted_iota(jnp.int32, scale.shape, 0)
    high = scale.astype(BF16).astype(F32)
    middle = (scale - high).astype(BF16).astype(F32)
    low = scale - high - middle
    value = jnp.where(row == 0, high, jnp.where(row == 1, middle, jnp.where(row == 2, low, 0.0)))
    tall = scale.shape[0]
    out_ref[:, : rows - tall, :] = codes_ref[...]
    out_ref[:, rows - tall :, :] = jnp.broadcast_to(value.astype(BF16)[None], (count, tall, lanes))


def reorder_kernel(owner_ref, returned_ref, out_ref):
    slab = out_ref.shape[1]
    rows, lanes = returned_ref.shape[1:]
    pieces = out_ref.shape[2] // lanes

    @pl.loop(0, out_ref.shape[0], unroll=16)
    def _(b):
        owner = owner_ref[b]
        scale = jnp.sum(returned_ref[owner, pieces * slab :, :].astype(F32), axis=0, keepdims=True)
        for i in range(pieces):
            value = decode(returned_ref[owner, i * slab : (i + 1) * slab, :])
            out_ref[b, :, i * lanes : (i + 1) * lanes] = value * scale


def per_device(grad_parts, block_owner, left_stat, right_stat, root_left, root_right):
    owners = lax.axis_size("fsdp")
    replicas = lax.axis_size("dp")
    me = lax.axis_index("dp")
    part, order = root_left.shape[1:]
    blocks, slab = grad_parts.shape[1:3]
    scale = (1.0 - AVERAGING) / order
    place = me.astype(jnp.int32).reshape(1)
    half = order // 2
    macs = 2 * 3 * part * part * order

    def shifted(value, k):
        return lax.ppermute(value, "dp", [(i, (i + k) % replicas) for i in range(replicas)])

    packed = call(
        pack_kernel,
        (like((blocks, slab, part), BF16),) * replicas,
        [place, grad_parts[0]],
        1,
    )
    arrived = [packed[0]] + [shifted(packed[k], k) for k in (2, 1, 3)]
    to_previous, to_next = call(
        root_pack_kernel,
        tuple(like((n, part, part // 2 * 3), BF16) for n in (3, 2)),
        [place, root_left[0]],
        1,
    )
    arrived, to_previous, to_next = lax.optimization_barrier((arrived, to_previous, to_next))
    root_after = shifted(to_previous, 3)
    root_before = shifted(to_next, 1)
    root_far = shifted(root_before[:1], 1)
    outgoing = call(
        sum_kernel, like((owners, slab, part // 2 * 3), BF16), [block_owner, *arrived], 1
    )
    own = lax.all_to_all(outgoing, "fsdp", split_axis=0, concat_axis=0, tiled=True)
    own = own.reshape(order, part // 2 * 3)
    own, root_after, root_before, root_far = lax.optimization_barrier(
        (own, root_after, root_before, root_far)
    )
    own = call(halves_kernel, (like((half, part // 2 * 3), BF16),) * 2, [own])

    before_top = shifted(own[0], 1)
    after_bottom = shifted(own[1], 3)
    before_bottom = shifted(own[1], 1)
    after_top = shifted(own[0], 3)
    far_top = shifted(before_top, 1)
    far_bottom = shifted(after_bottom, 3)

    def widened(value):
        return call(widen_kernel, like((half, 2 * part), BF16), [value])

    own = (widened(own[0]), widened(own[1]))
    before_top, before_bottom = widened(before_top), widened(before_bottom)
    after_top, after_bottom = widened(after_top), widened(after_bottom)
    root = root_right[0]
    own_square = call(square_kernel, like((8, 128)), [*own])
    stat = like((part, order))
    left, right = call(
        functools.partial(statistics_kernel, scale, (0,), True),
        (stat, stat),
        [place, *own, *own, left_stat[0], right_stat[0]],
        1,
        flops=2 * macs,
    )
    value = call(
        functools.partial(value_kernel, (0,), True),
        like((order, part)),
        [place, *own, root],
        1,
        flops=macs,
    )
    high, low = call(
        root_join_kernel,
        (like((order, order), BF16),) * 2,
        [place, root_left[0], root_after, root_before, root_far],
        1,
        cost=16 << 20,
    )
    near = (before_top, before_bottom, after_top, after_bottom)
    left, right = call(
        functools.partial(statistics_kernel, scale, (3, 1), False),
        (stat, stat),
        [place, *own, *near, left, right],
        1,
        flops=4 * macs,
    )
    value = call(
        functools.partial(value_kernel, (3, 1), False),
        like((order, part)),
        [place, *near, root, value],
        1,
        flops=2 * macs,
    )
    result, square, peak = call(
        functools.partial(result_kernel, 2),
        (like((order, part)), like((8, 128)), like((8, 128))),
        [place, far_top, far_bottom, root, value, high, low, own_square],
        1,
        flops=5 * macs,
    )
    squares = [square, shifted(square, 2), shifted(square, 1), shifted(square, 3)]
    codes = call(
        encode_kernel,
        like((owners, part * slab // 128, 128), BF16),
        [result, peak],
        cost=16 << 20,
    )
    codes = call(stamp_kernel, like((owners, part * slab // 128 + 8, 128), BF16), [peak, *squares, codes])
    returned = lax.all_to_all(codes, "fsdp", split_axis=0, concat_axis=0, tiled=True)
    left, right = call(
        functools.partial(statistics_kernel, scale, (2,), False),
        (stat, stat),
        [place, *own, widened(far_top), widened(far_bottom), left, right],
        1,
        flops=2 * macs,
    )
    direction = call(
        reorder_kernel, like((blocks, slab, part)), [block_owner, returned], 1
    )
    return (left[None], right[None], direction)


def solution(mesh):
    placed = (
        P("dp", None, "fsdp", None),
        P(),
        P("fsdp", "dp", None),
        P("fsdp", "dp", None),
        P("fsdp", "dp", None),
        P("fsdp", "dp", None),
    )
    return jax.shard_map(
        per_device,
        mesh=mesh,
        in_specs=placed,
        out_specs=(P("fsdp", "dp", None), P("fsdp", "dp", None), P(None, "fsdp", "dp")),
        check_vma=False,
    )
```

profile of v0, /device:TPU:1, one launch (start us, length us, event | category | flops | bytes accessed | tf_op | source)
XLA Modules:
  0.0 130.7 jit_solution(12925795981811899861)
XLA Ops:
  0.7 1.5 %copy-done.4 = bf16[1,48,16,1024]{3,2,1,0:T(8,128)(2,1)S(1)} copy-done((bf16[1,48,16,1024]{3,2,1,0:T(8,128)(2,1)S(1)}, bf16[1,48,16,1024]{3,2,1,0:T(8,128)(2,1)}, u32[]{:S(2)}) %copy-start.4) | copy-done | bytes 1572888
  2.1 0.2 shard_map.85
  2.3 3.8 %collective-permute-start = (bf16[48,16,256]{2,1,0:T(8,128)(2,1)S(1)}, bf16[48,16,256]{2,1,0:T(8,128)(2,1)S(1)}, u32[]{:S(2)}, u32[]{:S(2)}) collective-permute-start(bf16[48,16,256]{2,1,0:T(8,128)(2,1)S(1)} %get-tuple-element.33), channel_id=1, source_target_pairs={{0,2},{1,3},{2,0},{3,1},{4,6},{5,7},{6,4},{7,5},{8,10},{9,11},{10,... | collective-permute-start | bytes 1179656 | tf_op jit(solution)/shard_map/ppermute | solution.py:331
  6.2 0.4 collective-permute-start.1
  6.6 2.3 %collective-permute-start.2 = (bf16[48,16,256]{2,1,0:T(8,128)(2,1)S(1)}, bf16[48,16,256]{2,1,0:T(8,128)(2,1)S(1)}, u32[]{:S(2)}, u32[]{:S(2)}) collective-permute-start(bf16[48,16,256]{2,1,0:T(8,128)(2,1)S(1)} %get-tuple-element.35), channel_id=1, source_target_pairs={{0,3},{1,0},{2,1},{3,2},{4,7},{5,4},{6,5},{7,6},{8,11},{9,8},{10,9... | collective-permute-start | bytes 1179656 | tf_op jit(solution)/shard_map/ppermute | solution.py:331
  8.9 0.8 shard_map.86
  9.6 0.0 copy-start.12
  9.6 0.8 copy-done.12
  10.4 3.6 %collective-permute-done.refs_1_ = bf16[48,16,256]{2,1,0:T(8,128)(2,1)S(1)} collective-permute-done((bf16[48,16,256]{2,1,0:T(8,128)(2,1)S(1)}, bf16[48,16,256]{2,1,0:T(8,128)(2,1)S(1)}, u32[]{:S(2)}, u32[]{:S(2)}) %collective-permute-start) | collective-permute-done | bytes 393248 | tf_op jit(solution)/shard_map/ppermute | solution.py:331
  14.1 10.1 %collective-permute-done.1.refs_2_ = bf16[48,16,256]{2,1,0:T(8,128)(2,1)S(1)} collective-permute-done((bf16[48,16,256]{2,1,0:T(8,128)(2,1)S(1)}, bf16[48,16,256]{2,1,0:T(8,128)(2,1)S(1)}, u32[]{:S(2)}, u32[]{:S(2)}) %collective-permute-start.1) | collective-permute-done | bytes 393248 | tf_op jit(solution)/shard_map/ppermute | solution.py:331
  24.2 0.0 collective-permute-done.2.refs_3_
  24.2 2.2 %shard_map.87 = bf16[64,16,384]{2,1,0:T(8,128)(2,1)} custom-call(s32[48]{0:T(128)S(1)} %copy-done.11, bf16[48,16,256]{2,1,0:T(8,128)(2,1)S(1)} %get-tuple-element.38.refs_0_, bf16[48,16,256]{2,1,0:T(8,128)(2,1)S(1)} %collective-permute-done.refs_1_, bf16[48,16,256]{2,1,0:T(8,128)(2,1)S(1)} %collective-permute-done.1.refs_2_, ...), custom_call_target="tpu_custom_call" | custom-call | bytes 4194304 | tf_op jit(solution)/shard_map/pallas_call | solution.py:84
  26.4 12.4 %all-to-all-start = ((bf16[64,16,384]{2,1,0:T(8,128)(2,1)}), bf16[64,16,384]{2,1,0:T(8,128)(2,1)S(1)}, u32[]{:S(2)}, u32[]{:S(2)}) async-start(bf16[64,16,384]{2,1,0:T(8,128)(2,1)} %shard_map.87), calls=%async_computation | async-start | bytes 1572864 | tf_op jit(solution)/shard_map/all_to_all | solution.py:353
  38.8 1.2 collective-permute-start.4
  40.0 1.6 %collective-permute-start.3 = (bf16[3,256,384]{2,1,0:T(8,128)(2,1)}, bf16[3,256,384]{2,1,0:T(8,128)(2,1)S(1)}, u32[]{:S(2)}, u32[]{:S(2)}) collective-permute-start(bf16[3,256,384]{2,1,0:T(8,128)(2,1)} %copy-done.12), channel_id=1, source_target_pairs={{0,3},{1,0},{2,1},{3,2},{4,7},{5,4},{6,5},{7,6},{8,11},{9,8},{10,9... | collective-permute-start | bytes 1769480 | tf_op jit(solution)/shard_map/ppermute | solution.py:331
  41.6 8.8 %collective-permute-done.4.before_ref = bf16[2,256,384]{2,1,0:T(8,128)(2,1)S(1)} collective-permute-done((bf16[2,256,384]{2,1,0:T(8,128)(2,1)S(1)}, bf16[2,256,384]{2,1,0:T(8,128)(2,1)S(1)}, u32[]{:S(2)}, u32[]{:S(2)}) %collective-permute-start.4) | collective-permute-done | bytes 393248 | tf_op jit(solution)/shard_map/ppermute | solution.py:331
  50.4 0.1 collective-permute-start.5
  50.5 6.3 %collective-permute-done.5.far_ref = bf16[1,256,384]{2,1,0:T(8,128)(2,1)S(1)} collective-permute-done((bf16[1,256,384]{2,1,0:T(8,128)(2,1)S(1)}, bf16[1,256,384]{2,1,0:T(8,128)(2,1)S(1)}, u32[]{:S(2)}, u32[]{:S(2)}) %collective-permute-start.5) | collective-permute-done | bytes 196640 | tf_op jit(solution)/shard_map/ppermute | solution.py:331
  56.8 0.0 collective-permute-done.3.after_ref
  56.8 5.0 %all-to-all-done = bf16[64,16,384]{2,1,0:T(8,128)(2,1)S(1)} async-done(((bf16[64,16,384]{2,1,0:T(8,128)(2,1)}), bf16[64,16,384]{2,1,0:T(8,128)(2,1)S(1)}, u32[]{:S(2)}, u32[]{:S(2)}) %all-to-all-start) | async-done | bytes 786464 | tf_op jit(solution)/shard_map/all_to_all | solution.py:353
  61.8 0.1 shard_map.88
  61.9 1.2 collective-permute-start.6
  63.0 1.6 %collective-permute-start.8 = (bf16[512,384]{1,0:T(8,128)(2,1)S(1)}, bf16[512,384]{1,0:T(8,128)(2,1)S(1)}, u32[]{:S(2)}, u32[]{:S(2)}) collective-permute-start(bf16[512,384]{1,0:T(8,128)(2,1)S(1)} %get-tuple-element.46.part_ref), channel_id=1, source_target_pairs={{0,3},{1,0},{2,1},{3,2},{4,7},{5,4},{6,5},{7,6},{8,11},{9,8},{10,9... | collective-permute-start | bytes 1179656 | tf_op jit(solution)/shard_map/ppermute | solution.py:331
  64.6 0.0 collective-permute-start.10
  64.6 2.7 %collective-permute-start.11 = (bf16[512,384]{1,0:T(8,128)(2,1)S(1)}, bf16[512,384]{1,0:T(8,128)(2,1)S(1)}, u32[]{:S(2)}, u32[]{:S(2)}) collective-permute-start(bf16[512,384]{1,0:T(8,128)(2,1)S(1)} %get-tuple-element.45.part_ref), channel_id=1, source_target_pairs={{0,3},{1,0},{2,1},{3,2},{4,7},{5,4},{6,5},{7,6},{8,11},{9,8},{10,9... | collective-permute-start | bytes 1179656 | tf_op jit(solution)/shard_map/ppermute | solution.py:331
  67.3 6.2 %collective-permute-done.6.part_ref = bf16[512,384]{1,0:T(8,128)(2,1)S(1)} collective-permute-done((bf16[512,384]{1,0:T(8,128)(2,1)S(1)}, bf16[512,384]{1,0:T(8,128)(2,1)S(1)}, u32[]{:S(2)}, u32[]{:S(2)}) %collective-permute-start.6) | collective-permute-done | bytes 393248 | tf_op jit(solution)/shard_map/ppermute | solution.py:331
  73.5 0.0 collective-permute-start.7
  73.5 0.0 collective-permute-done.8.part_ref
  73.5 2.7 %collective-permute-start.9 = (bf16[512,384]{1,0:T(8,128)(2,1)S(1)}, bf16[512,384]{1,0:T(8,128)(2,1)S(1)}, u32[]{:S(2)}, u32[]{:S(2)}) collective-permute-start(bf16[512,384]{1,0:T(8,128)(2,1)S(1)} %collective-permute-done.8.part_ref), channel_id=1, source_target_pairs={{0,3},{1,0},{2,1},{3,2},{4,7},{5,4},{6,5},{7,6},{8,11},{9,8},{10,9... | collective-permute-start | bytes 1179656 | tf_op jit(solution)/shard_map/ppermute | solution.py:331
  76.1 0.3 shard_map.89.refs_0_.refs_2_.top_ref
  76.4 0.0 copy-start.1
  76.4 0.3 shard_map.90.refs_1_.refs_3_.bottom_ref
  76.7 0.3 shard_map.103.own_square
  77.0 1.4 %shard_map.102 = (bf16[1024,1024]{1,0:T(8,128)(2,1)S(1)}, bf16[1024,1024]{1,0:T(8,128)(2,1)S(1)}) custom-call(s32[1]{0:T(128)} %bitcast.place_ref, f32[256,1024]{1,0:T(8,128)S(1)} %bitcast.10, bf16[3,256,384]{2,1,0:T(8,128)(2,1)S(1)} %collective-permute-done.3.after_ref, bf16[2,256,384]{2,1,0:T(8,128)(2,1)S(1)} %collective-permute-done.4.before_ref, ...), custom_call_target="tpu_custom_call" | custom-call | bytes 16777216 | tf_op jit(solution)/shard_map/pallas_call | solution.py:84
  78.5 0.6 shard_map.100.refs_5_
  79.1 0.3 shard_map.93.refs_2_.refs_0_
  79.3 0.3 shard_map.96.refs_5_.refs_3_
  79.6 2.3 %collective-permute-done.10.part_ref = bf16[512,384]{1,0:T(8,128)(2,1)S(1)} collective-permute-done((bf16[512,384]{1,0:T(8,128)(2,1)S(1)}, bf16[512,384]{1,0:T(8,128)(2,1)S(1)}, u32[]{:S(2)}, u32[]{:S(2)}) %collective-permute-start.10) | collective-permute-done | bytes 393248 | tf_op jit(solution)/shard_map/ppermute | solution.py:331
  81.9 0.3 shard_map.94.refs_3_.refs_1_
  82.1 0.0 collective-permute-done.11.part_ref
  82.1 0.3 shard_map.95.refs_4_.refs_2_
  82.4 0.0 copy-start.2
  82.4 1.0 shard_map.101.value_ref
  83.5 6.8 %collective-permute-done.7.part_ref.top_ref = bf16[512,384]{1,0:T(8,128)(2,1)S(1)} collective-permute-done((bf16[512,384]{1,0:T(8,128)(2,1)S(1)}, bf16[512,384]{1,0:T(8,128)(2,1)S(1)}, u32[]{:S(2)}, u32[]{:S(2)}) %collective-permute-start.7) | collective-permute-done | bytes 393248 | tf_op jit(solution)/shard_map/ppermute | solution.py:331
  90.3 0.0 collective-permute-done.9.part_ref.bottom_ref
  90.3 2.7 %shard_map.104 = (f32[1024,256]{1,0:T(8,128)S(1)}, f32[8,128]{1,0:T(8,128)S(1)}, f32[8,128]{1,0:T(8,128)S(1)}) custom-call(s32[1]{0:T(128)} %bitcast.place_ref, bf16[512,384]{1,0:T(8,128)(2,1)S(1)} %collective-permute-done.7.part_ref.top_ref, bf16[512,384]{1,0:T(8,128)(2,1)S(1)} %collective-permute-done.9.part_ref.bottom_ref, f32[256,1024]{1,0:T(8,128)S(1)} %bitcast.13, ...), custom_call_target="tpu_custom_call" | custom-call | flops 2013265920 | bytes 4194304 | tf_op jit(solution)/shard_map/pallas_call | solution.py:84
  93.1 2.1 %collective-permute-start.12 = (f32[8,128]{1,0:T(8,128)S(1)}, f32[8,128]{1,0:T(8,128)S(1)}, u32[]{:S(2)}, u32[]{:S(2)}) collective-permute-start(f32[8,128]{1,0:T(8,128)S(1)} %get-tuple-element.59.refs_0_), channel_id=1, source_target_pairs={{0,2},{1,3},{2,0},{3,1},{4,6},{5,7},{6,4},{7,5},{8,10},{9,11},{10,... | collective-permute-start | bytes 12296 | tf_op jit(solution)/shard_map/ppermute | solution.py:331
  95.1 0.9 collective-permute-start.13
  96.1 1.7 %collective-permute-start.14 = (f32[8,128]{1,0:T(8,128)S(1)}, f32[8,128]{1,0:T(8,128)S(1)}, u32[]{:S(2)}, u32[]{:S(2)}) collective-permute-start(f32[8,128]{1,0:T(8,128)S(1)} %get-tuple-element.59.refs_0_), channel_id=1, source_target_pairs={{0,3},{1,0},{2,1},{3,2},{4,7},{5,4},{6,5},{7,6},{8,11},{9,8},{10,9... | collective-permute-start | bytes 12296 | tf_op jit(solution)/shard_map/ppermute | solution.py:331
  97.8 1.1 shard_map.105.refs_4_
  98.9 0.2 collective-permute-done.13.refs_2_
  99.1 1.0 shard_map.106
  100.1 8.3 %all-to-all-start.1 = ((bf16[64,40,128]{2,1,0:T(8,128)(2,1)}), bf16[64,40,128]{2,1,0:T(8,128)(2,1)S(1)}, u32[]{:S(2)}, u32[]{:S(2)}) async-start(bf16[64,40,128]{2,1,0:T(8,128)(2,1)} %shard_map.106), calls=%async_computation.1 | async-start | bytes 1310720 | tf_op jit(solution)/shard_map/all_to_all | solution.py:427
  108.4 0.0 copy-start.5
  108.4 1.2 copy-done.5
  109.6 1.2 copy-done.6
  110.9 1.2 shard_map.97
  112.0 0.0 copy-start.8
  112.1 1.9 %shard_map.98 = (f32[256,1024]{1,0:T(8,128)S(1)}, f32[256,1024]{1,0:T(8,128)S(1)}) custom-call(s32[1]{0:T(128)} %bitcast.place_ref, bf16[512,512]{1,0:T(8,128)(2,1)S(1)} %shard_map.89.refs_0_.refs_2_.top_ref, bf16[512,512]{1,0:T(8,128)(2,1)S(1)} %shard_map.90.refs_1_.refs_3_.bottom_ref, bf16[512,512]{1,0:T(8,128)(2,1)S(1)} %shard_map.93.refs_2_.refs_0_, ...), custom_call_target="tpu_custom_call" | custom-call | flops 1610612736 | bytes 4194304 | tf_op jit(solution)/shard_map/pallas_call | solution.py:84
  114.0 0.3 shard_map.91.refs_2_
  114.3 0.3 shard_map.92.refs_3_
  114.5 2.3 %shard_map.99 = (f32[256,1024]{1,0:T(8,128)}, f32[256,1024]{1,0:T(8,128)}) custom-call(s32[1]{0:T(128)} %bitcast.place_ref, bf16[512,512]{1,0:T(8,128)(2,1)S(1)} %shard_map.89.refs_0_.refs_2_.top_ref, bf16[512,512]{1,0:T(8,128)(2,1)S(1)} %shard_map.90.refs_1_.refs_3_.bottom_ref, bf16[512,512]{1,0:T(8,128)(2,1)S(1)} %shard_map.91.refs_2_, ...), custom_call_target="tpu_custom_call" | custom-call | flops 805306368 | bytes 4194304 | tf_op jit(solution)/shard_map/pallas_call | solution.py:84
  116.8 11.7 %all-to-all-done.1.returned_ref = bf16[64,40,128]{2,1,0:T(8,128)(2,1)S(1)} async-done(((bf16[64,40,128]{2,1,0:T(8,128)(2,1)}), bf16[64,40,128]{2,1,0:T(8,128)(2,1)S(1)}, u32[]{:S(2)}, u32[]{:S(2)}) %all-to-all-start.1) | async-done | bytes 655392 | tf_op jit(solution)/shard_map/all_to_all | solution.py:427
  128.5 2.1 %shard_map.107 = f32[48,16,256]{2,1,0:T(8,128)} custom-call(s32[48]{0:T(128)S(1)} %copy-done.11, bf16[64,40,128]{2,1,0:T(8,128)(2,1)S(1)} %all-to-all-done.1.returned_ref), custom_call_target="tpu_custom_call" | custom-call | bytes 4194304 | tf_op jit(solution)/shard_map/pallas_call | solution.py:84
  (20 shorter events, 0.1 us)
Async XLA Ops:
  0.6 8.2 %copy-start = (f32[1,256,1024]{2,1,0:T(8,128)S(1)}, f32[1,256,1024]{2,1,0:T(8,128)}, u32[]{:S(2)}) copy-start(f32[1,256,1024]{2,1,0:T(8,128)} %param.10) | copy-start | bytes 3145732
  0.6 1.5 %copy-start.4 = (bf16[1,48,16,1024]{3,2,1,0:T(8,128)(2,1)S(1)}, bf16[1,48,16,1024]{3,2,1,0:T(8,128)(2,1)}, u32[]{:S(2)}) copy-start(bf16[1,48,16,1024]{3,2,1,0:T(8,128)(2,1)} %param.6) | copy-start | bytes 4718596
  2.1 22.0 %copy-start.11 = (s32[48]{0:T(128)S(1)}, s32[48]{0:T(128)}, u32[]{:S(2)}) copy-start(s32[48]{0:T(128)} %owner_ref.3) | copy-start | bytes 580
  2.3 11.7 %collective-permute-start = (bf16[48,16,256]{2,1,0:T(8,128)(2,1)S(1)}, bf16[48,16,256]{2,1,0:T(8,128)(2,1)S(1)}, u32[]{:S(2)}, u32[]{:S(2)}) collective-permute-start(bf16[48,16,256]{2,1,0:T(8,128)(2,1)S(1)} %get-tuple-element.33), channel_id=1, source_target_pairs={{0,2},{1,3},{2,0},{3,1},{4,6},{5,7},{6,4},{7,5},{8,10},{9,11},{10,... | collective-permute-start | bytes 1179656 | tf_op jit(solution)/shard_map/ppermute | solution.py:331
  6.2 18.0 %collective-permute-start.1 = (bf16[48,16,256]{2,1,0:T(8,128)(2,1)S(1)}, bf16[48,16,256]{2,1,0:T(8,128)(2,1)S(1)}, u32[]{:S(2)}, u32[]{:S(2)}) collective-permute-start(bf16[48,16,256]{2,1,0:T(8,128)(2,1)S(1)} %get-tuple-element.34), channel_id=1, source_target_pairs={{0,1},{1,2},{2,3},{3,0},{4,5},{5,6},{6,7},{7,4},{8,9},{9,10},{10,1... | collective-permute-start | bytes 1179656 | tf_op jit(solution)/shard_map/ppermute | solution.py:331
  6.6 17.6 %collective-permute-start.2 = (bf16[48,16,256]{2,1,0:T(8,128)(2,1)S(1)}, bf16[48,16,256]{2,1,0:T(8,128)(2,1)S(1)}, u32[]{:S(2)}, u32[]{:S(2)}) collective-permute-start(bf16[48,16,256]{2,1,0:T(8,128)(2,1)S(1)} %get-tuple-element.35), channel_id=1, source_target_pairs={{0,3},{1,0},{2,1},{3,2},{4,7},{5,4},{6,5},{7,6},{8,11},{9,8},{10,9... | collective-permute-start | bytes 1179656 | tf_op jit(solution)/shard_map/ppermute | solution.py:331
  9.6 0.8 copy-start.12
  26.4 35.4 %all-to-all-start = ((bf16[64,16,384]{2,1,0:T(8,128)(2,1)}), bf16[64,16,384]{2,1,0:T(8,128)(2,1)S(1)}, u32[]{:S(2)}, u32[]{:S(2)}) async-start(bf16[64,16,384]{2,1,0:T(8,128)(2,1)} %shard_map.87), calls=%async_computation | async-start | bytes 1572864 | tf_op jit(solution)/shard_map/all_to_all | solution.py:353
  38.8 11.5 %collective-permute-start.4 = (bf16[2,256,384]{2,1,0:T(8,128)(2,1)S(1)}, bf16[2,256,384]{2,1,0:T(8,128)(2,1)S(1)}, u32[]{:S(2)}, u32[]{:S(2)}) collective-permute-start(bf16[2,256,384]{2,1,0:T(8,128)(2,1)S(1)} %get-tuple-element.43), channel_id=1, source_target_pairs={{0,1},{1,2},{2,3},{3,0},{4,5},{5,6},{6,7},{7,4},{8,9},{9,10},{10,1... | collective-permute-start | bytes 1179656 | tf_op jit(solution)/shard_map/ppermute | solution.py:331
  40.0 16.8 %collective-permute-start.3 = (bf16[3,256,384]{2,1,0:T(8,128)(2,1)}, bf16[3,256,384]{2,1,0:T(8,128)(2,1)S(1)}, u32[]{:S(2)}, u32[]{:S(2)}) collective-permute-start(bf16[3,256,384]{2,1,0:T(8,128)(2,1)} %copy-done.12), channel_id=1, source_target_pairs={{0,3},{1,0},{2,1},{3,2},{4,7},{5,4},{6,5},{7,6},{8,11},{9,8},{10,9... | collective-permute-start | bytes 1769480 | tf_op jit(solution)/shard_map/ppermute | solution.py:331
  50.4 6.4 %collective-permute-start.5 = (bf16[1,256,384]{2,1,0:T(8,128)(2,1)S(1)}, bf16[1,256,384]{2,1,0:T(8,128)(2,1)S(1)}, u32[]{:S(2)}, u32[]{:S(2)}) collective-permute-start(bf16[1,256,384]{2,1,0:T(8,128)(2,1)S(1)} %slice.4), channel_id=1, source_target_pairs={{0,1},{1,2},{2,3},{3,0},{4,5},{5,6},{6,7},{7,4},{8,9},{9,10},{10,1... | collective-permute-start | bytes 589832 | tf_op jit(solution)/shard_map/ppermute | solution.py:331
  61.9 11.6 %collective-permute-start.6 = (bf16[512,384]{1,0:T(8,128)(2,1)S(1)}, bf16[512,384]{1,0:T(8,128)(2,1)S(1)}, u32[]{:S(2)}, u32[]{:S(2)}) collective-permute-start(bf16[512,384]{1,0:T(8,128)(2,1)S(1)} %get-tuple-element.45.part_ref), channel_id=1, source_target_pairs={{0,1},{1,2},{2,3},{3,0},{4,5},{5,6},{6,7},{7,4},{8,9},{9,10},{10,1... | collective-permute-start | bytes 1179656 | tf_op jit(solution)/shard_map/ppermute | solution.py:331
  63.0 10.4 %collective-permute-start.8 = (bf16[512,384]{1,0:T(8,128)(2,1)S(1)}, bf16[512,384]{1,0:T(8,128)(2,1)S(1)}, u32[]{:S(2)}, u32[]{:S(2)}) collective-permute-start(bf16[512,384]{1,0:T(8,128)(2,1)S(1)} %get-tuple-element.46.part_ref), channel_id=1, source_target_pairs={{0,3},{1,0},{2,1},{3,2},{4,7},{5,4},{6,5},{7,6},{8,11},{9,8},{10,9... | collective-permute-start | bytes 1179656 | tf_op jit(solution)/shard_map/ppermute | solution.py:331
  64.6 17.3 %collective-permute-start.10 = (bf16[512,384]{1,0:T(8,128)(2,1)S(1)}, bf16[512,384]{1,0:T(8,128)(2,1)S(1)}, u32[]{:S(2)}, u32[]{:S(2)}) collective-permute-start(bf16[512,384]{1,0:T(8,128)(2,1)S(1)} %get-tuple-element.46.part_ref), channel_id=1, source_target_pairs={{0,1},{1,2},{2,3},{3,0},{4,5},{5,6},{6,7},{7,4},{8,9},{9,10},{10,1... | collective-permute-start | bytes 1179656 | tf_op jit(solution)/shard_map/ppermute | solution.py:331
  64.6 17.5 %collective-permute-start.11 = (bf16[512,384]{1,0:T(8,128)(2,1)S(1)}, bf16[512,384]{1,0:T(8,128)(2,1)S(1)}, u32[]{:S(2)}, u32[]{:S(2)}) collective-permute-start(bf16[512,384]{1,0:T(8,128)(2,1)S(1)} %get-tuple-element.45.part_ref), channel_id=1, source_target_pairs={{0,3},{1,0},{2,1},{3,2},{4,7},{5,4},{6,5},{7,6},{8,11},{9,8},{10,9... | collective-permute-start | bytes 1179656 | tf_op jit(solution)/shard_map/ppermute | solution.py:331
  73.5 16.9 %collective-permute-start.7 = (bf16[512,384]{1,0:T(8,128)(2,1)S(1)}, bf16[512,384]{1,0:T(8,128)(2,1)S(1)}, u32[]{:S(2)}, u32[]{:S(2)}) collective-permute-start(bf16[512,384]{1,0:T(8,128)(2,1)S(1)} %collective-permute-done.6.part_ref), channel_id=1, source_target_pairs={{0,1},{1,2},{2,3},{3,0},{4,5},{5,6},{6,7},{7,4},{8,9},{9,10},{10,1... | collective-permute-start | bytes 1179656 | tf_op jit(solution)/shard_map/ppermute | solution.py:331
  73.5 16.9 %collective-permute-start.9 = (bf16[512,384]{1,0:T(8,128)(2,1)S(1)}, bf16[512,384]{1,0:T(8,128)(2,1)S(1)}, u32[]{:S(2)}, u32[]{:S(2)}) collective-permute-start(bf16[512,384]{1,0:T(8,128)(2,1)S(1)} %collective-permute-done.8.part_ref), channel_id=1, source_target_pairs={{0,3},{1,0},{2,1},{3,2},{4,7},{5,4},{6,5},{7,6},{8,11},{9,8},{10,9... | collective-permute-start | bytes 1179656 | tf_op jit(solution)/shard_map/ppermute | solution.py:331
  76.4 2.1 %copy-start.1 = (f32[1,256,1024]{2,1,0:T(8,128)S(1)}, f32[1,256,1024]{2,1,0:T(8,128)}, u32[]{:S(2)}) copy-start(f32[1,256,1024]{2,1,0:T(8,128)} %param.11) | copy-start | bytes 3145732
  82.4 1.0 copy-start.2
  90.3 2.7 %copy-start.7 = (bf16[512,384]{1,0:T(8,128)(2,1)}, bf16[512,384]{1,0:T(8,128)(2,1)S(1)}, u32[]{:S(2)}) copy-start(bf16[512,384]{1,0:T(8,128)(2,1)S(1)} %collective-permute-done.7.part_ref.top_ref) | copy-start | bytes 1179652
  90.3 2.7 %copy-start.9 = (bf16[512,384]{1,0:T(8,128)(2,1)}, bf16[512,384]{1,0:T(8,128)(2,1)S(1)}, u32[]{:S(2)}) copy-start(bf16[512,384]{1,0:T(8,128)(2,1)S(1)} %collective-permute-done.9.part_ref.bottom_ref) | copy-start | bytes 1179652
  93.1 5.9 %collective-permute-start.12 = (f32[8,128]{1,0:T(8,128)S(1)}, f32[8,128]{1,0:T(8,128)S(1)}, u32[]{:S(2)}, u32[]{:S(2)}) collective-permute-start(f32[8,128]{1,0:T(8,128)S(1)} %get-tuple-element.59.refs_0_), channel_id=1, source_target_pairs={{0,2},{1,3},{2,0},{3,1},{4,6},{5,7},{6,4},{7,5},{8,10},{9,11},{10,... | collective-permute-start | bytes 12296 | tf_op jit(solution)/shard_map/ppermute | solution.py:331
  95.1 4.0 %collective-permute-start.13 = (f32[8,128]{1,0:T(8,128)S(1)}, f32[8,128]{1,0:T(8,128)S(1)}, u32[]{:S(2)}, u32[]{:S(2)}) collective-permute-start(f32[8,128]{1,0:T(8,128)S(1)} %get-tuple-element.59.refs_0_), channel_id=1, source_target_pairs={{0,1},{1,2},{2,3},{3,0},{4,5},{5,6},{6,7},{7,4},{8,9},{9,10},{10,1... | collective-permute-start | bytes 12296 | tf_op jit(solution)/shard_map/ppermute | solution.py:331
  96.1 3.0 %collective-permute-start.14 = (f32[8,128]{1,0:T(8,128)S(1)}, f32[8,128]{1,0:T(8,128)S(1)}, u32[]{:S(2)}, u32[]{:S(2)}) collective-permute-start(f32[8,128]{1,0:T(8,128)S(1)} %get-tuple-element.59.refs_0_), channel_id=1, source_target_pairs={{0,3},{1,0},{2,1},{3,2},{4,7},{5,4},{6,5},{7,6},{8,11},{9,8},{10,9... | collective-permute-start | bytes 12296 | tf_op jit(solution)/shard_map/ppermute | solution.py:331
  100.1 28.4 %all-to-all-start.1 = ((bf16[64,40,128]{2,1,0:T(8,128)(2,1)}), bf16[64,40,128]{2,1,0:T(8,128)(2,1)S(1)}, u32[]{:S(2)}, u32[]{:S(2)}) async-start(bf16[64,40,128]{2,1,0:T(8,128)(2,1)} %shard_map.106), calls=%async_computation.1 | async-start | bytes 1310720 | tf_op jit(solution)/shard_map/all_to_all | solution.py:427
  108.4 1.2 copy-start.5
  109.6 1.2 copy-start.6
  110.9 1.2 copy-start.3
  112.0 1.9 %copy-start.8 = (bf16[512,384]{1,0:T(8,128)(2,1)S(1)}, bf16[512,384]{1,0:T(8,128)(2,1)}, u32[]{:S(2)}) copy-start(bf16[512,384]{1,0:T(8,128)(2,1)} %copy-done.7) | copy-start | bytes 1179652
  112.0 2.2 %copy-start.10 = (bf16[512,384]{1,0:T(8,128)(2,1)S(1)}, bf16[512,384]{1,0:T(8,128)(2,1)}, u32[]{:S(2)}) copy-start(bf16[512,384]{1,0:T(8,128)(2,1)} %copy-done.9) | copy-start | bytes 1179652
where the time goes:
time: 131 us
  waiting for transfers between devices  61 us (47%)
  starting transfers between devices  42.9 us (33%)
  Pallas kernels  21 us (16%)
  local copies, waits for them, and re-layouts  4.8 us (4%)
    ppermute x15, waiting for transfers between devices, shifted(): lax.ppermute(value, 'dp', [(i, (i + k) % replicas) for i in range(replica...  44.3 us
    ppermute x15, starting transfers between devices, shifted(): lax.ppermute(value, 'dp', [(i, (i + k) % replicas) for i in range(replica...  22.2 us
    pallas_call x23, Pallas kernels, call(): pl.pallas_call(kernel, out_shape=outs, in_specs=[SMEM] * n_smem + [VMEM]...  21 us
    all_to_all x1, starting transfers between devices, per_device(): lax.all_to_all(outgoing, 'fsdp', split_axis=0, concat_axis=0, tiled=True)  12.4 us
    all_to_all x1, waiting for transfers between devices, per_device(): lax.all_to_all(codes, 'fsdp', split_axis=0, concat_axis=0, tiled=True)  11.7 us
    all_to_all x1, starting transfers between devices, per_device(): lax.all_to_all(codes, 'fsdp', split_axis=0, concat_axis=0, tiled=True)  8.29 us
    all_to_all x1, waiting for transfers between devices, per_device(): lax.all_to_all(outgoing, 'fsdp', split_axis=0, concat_axis=0, tiled=True)  5.04 us
    unnamed x26, local copies, waits for them, and re-layouts  4.78 us
  transfers between devices with their start and end apart: 17, of which 10 were waited for; matrix products, arithmetic and copies ran while one was open for 0% of the time, Pallas kernels for 10%

commit v1 on v0

--- a/solution.py
+++ b/solution.py
@@ -259,7 +259,6 @@
 
 
 def decode(number):
-    number = number.astype(F32)
     size = jnp.abs(number)
     exponent = jnp.floor(jnp.log(jnp.maximum(size, 2e-38)) * (1.0 / math.log(2.0)) + 0.002)
     root = jnp.exp2(exponent * -0.5)
@@ -289,7 +288,6 @@
     total = square_refs[0][...]
     for ref in square_refs[1:]:
         total = total + ref[...]
-    count, rows, lanes = out_ref.shape
     gradient, result = total[:, :1], total[:, 1:2]
     scale = peak_ref[...] * (jnp.sqrt(gradient) * lax.rsqrt(result + GRAFT_EPS))
     row = lax.broadcasted_iota(jnp.int32, scale.shape, 0)
@@ -297,22 +295,24 @@
     middle = (scale - high).astype(BF16).astype(F32)
     low = scale - high - middle
     value = jnp.where(row == 0, high, jnp.where(row == 1, middle, jnp.where(row == 2, low, 0.0)))
-    tall = scale.shape[0]
-    out_ref[:, : rows - tall, :] = codes_ref[...]
-    out_ref[:, rows - tall :, :] = jnp.broadcast_to(value.astype(BF16)[None], (count, tall, lanes))
+
+    @pl.loop(0, out_ref.shape[0], unroll=8)
+    def _(o):
+        packet = jnp.concatenate([codes_ref[o].astype(F32), value], axis=0)
+        out_ref[o] = packet.astype(BF16)
 
 
 def reorder_kernel(owner_ref, returned_ref, out_ref):
     slab = out_ref.shape[1]
-    rows, lanes = returned_ref.shape[1:]
+    lanes = returned_ref.shape[2]
     pieces = out_ref.shape[2] // lanes
 
     @pl.loop(0, out_ref.shape[0], unroll=16)
     def _(b):
-        owner = owner_ref[b]
-        scale = jnp.sum(returned_ref[owner, pieces * slab :, :].astype(F32), axis=0, keepdims=True)
+        packet = returned_ref[owner_ref[b]].astype(F32)
+        scale = jnp.sum(packet[pieces * slab :], axis=0, keepdims=True)
         for i in range(pieces):
-            value = decode(returned_ref[owner, i * slab : (i + 1) * slab, :])
+            value = decode(packet[i * slab : (i + 1) * slab])
             out_ref[b, :, i * lanes : (i + 1) * lanes] = value * scale
 
 

time: 131 us -> 131 us (level)
  no operation moved by 1% of the time
where the time goes in v1:
time: 131 us
  waiting for transfers between devices  61 us (47%)
  starting transfers between devices  42.9 us (33%)
  Pallas kernels  21.1 us (16%)
  local copies, waits for them, and re-layouts  4.8 us (4%)
    ppermute x15, waiting for transfers between devices, shifted(): lax.ppermute(value, 'dp', [(i, (i + k) % replicas) for i in range(replica...  44.3 us
    ppermute x15, starting transfers between devices, shifted(): lax.ppermute(value, 'dp', [(i, (i + k) % replicas) for i in range(replica...  22.2 us
    pallas_call x23, Pallas kernels, call(): pl.pallas_call(kernel, out_shape=outs, in_specs=[SMEM] * n_smem + [VMEM]...  21.1 us
    all_to_all x1, starting transfers between devices, per_device(): lax.all_to_all(outgoing, 'fsdp', split_axis=0, concat_axis=0, tiled=True)  12.4 us
    all_to_all x1, waiting for transfers between devices, per_device(): lax.all_to_all(codes, 'fsdp', split_axis=0, concat_axis=0, tiled=True)  11.7 us
    all_to_all x1, starting transfers between devices, per_device(): lax.all_to_all(codes, 'fsdp', split_axis=0, concat_axis=0, tiled=True)  8.29 us
    all_to_all x1, waiting for transfers between devices, per_device(): lax.all_to_all(outgoing, 'fsdp', split_axis=0, concat_axis=0, tiled=True)  5.04 us
    unnamed x26, local copies, waits for them, and re-layouts  4.78 us
  transfers between devices with their start and end apart: 17, of which 10 were waited for; matrix products, arithmetic and copies ran while one was open for 0% of the time, Pallas kernels for 10%

profile of v1, /device:TPU:1, one launch (start us, length us, event | category | flops | bytes accessed | tf_op | source)
XLA Modules:
  0.0 130.8 jit_solution(14819545309270917500)
XLA Ops:
  0.7 1.5 %copy-done.4 = bf16[1,48,16,1024]{3,2,1,0:T(8,128)(2,1)S(1)} copy-done((bf16[1,48,16,1024]{3,2,1,0:T(8,128)(2,1)S(1)}, bf16[1,48,16,1024]{3,2,1,0:T(8,128)(2,1)}, u32[]{:S(2)}) %copy-start.4) | copy-done | bytes 1572888
  2.1 0.2 shard_map.85
  2.3 3.8 %collective-permute-start = (bf16[48,16,256]{2,1,0:T(8,128)(2,1)S(1)}, bf16[48,16,256]{2,1,0:T(8,128)(2,1)S(1)}, u32[]{:S(2)}, u32[]{:S(2)}) collective-permute-start(bf16[48,16,256]{2,1,0:T(8,128)(2,1)S(1)} %get-tuple-element.33), channel_id=1, source_target_pairs={{0,2},{1,3},{2,0},{3,1},{4,6},{5,7},{6,4},{7,5},{8,10},{9,11},{10,... | collective-permute-start | bytes 1179656 | tf_op jit(solution)/shard_map/ppermute | solution.py:331
  6.2 0.4 collective-permute-start.1
  6.6 2.3 %collective-permute-start.2 = (bf16[48,16,256]{2,1,0:T(8,128)(2,1)S(1)}, bf16[48,16,256]{2,1,0:T(8,128)(2,1)S(1)}, u32[]{:S(2)}, u32[]{:S(2)}) collective-permute-start(bf16[48,16,256]{2,1,0:T(8,128)(2,1)S(1)} %get-tuple-element.35), channel_id=1, source_target_pairs={{0,3},{1,0},{2,1},{3,2},{4,7},{5,4},{6,5},{7,6},{8,11},{9,8},{10,9... | collective-permute-start | bytes 1179656 | tf_op jit(solution)/shard_map/ppermute | solution.py:331
  8.9 0.8 shard_map.86
  9.6 0.0 copy-start.12
  9.6 0.8 copy-done.12
  10.4 3.6 %collective-permute-done.refs_1_ = bf16[48,16,256]{2,1,0:T(8,128)(2,1)S(1)} collective-permute-done((bf16[48,16,256]{2,1,0:T(8,128)(2,1)S(1)}, bf16[48,16,256]{2,1,0:T(8,128)(2,1)S(1)}, u32[]{:S(2)}, u32[]{:S(2)}) %collective-permute-start) | collective-permute-done | bytes 393248 | tf_op jit(solution)/shard_map/ppermute | solution.py:331
  14.1 10.1 %collective-permute-done.1.refs_2_ = bf16[48,16,256]{2,1,0:T(8,128)(2,1)S(1)} collective-permute-done((bf16[48,16,256]{2,1,0:T(8,128)(2,1)S(1)}, bf16[48,16,256]{2,1,0:T(8,128)(2,1)S(1)}, u32[]{:S(2)}, u32[]{:S(2)}) %collective-permute-start.1) | collective-permute-done | bytes 393248 | tf_op jit(solution)/shard_map/ppermute | solution.py:331
  24.2 0.0 collective-permute-done.2.refs_3_
  24.2 2.2 %shard_map.87 = bf16[64,16,384]{2,1,0:T(8,128)(2,1)} custom-call(s32[48]{0:T(128)S(1)} %copy-done.11, bf16[48,16,256]{2,1,0:T(8,128)(2,1)S(1)} %get-tuple-element.38.refs_0_, bf16[48,16,256]{2,1,0:T(8,128)(2,1)S(1)} %collective-permute-done.refs_1_, bf16[48,16,256]{2,1,0:T(8,128)(2,1)S(1)} %collective-permute-done.1.refs_2_, ...), custom_call_target="tpu_custom_call" | custom-call | bytes 4194304 | tf_op jit(solution)/shard_map/pallas_call | solution.py:84
  26.4 12.4 %all-to-all-start = ((bf16[64,16,384]{2,1,0:T(8,128)(2,1)}), bf16[64,16,384]{2,1,0:T(8,128)(2,1)S(1)}, u32[]{:S(2)}, u32[]{:S(2)}) async-start(bf16[64,16,384]{2,1,0:T(8,128)(2,1)} %shard_map.87), calls=%async_computation | async-start | bytes 1572864 | tf_op jit(solution)/shard_map/all_to_all | solution.py:353
  38.8 1.2 collective-permute-start.4
  40.0 1.6 %collective-permute-start.3 = (bf16[3,256,384]{2,1,0:T(8,128)(2,1)}, bf16[3,256,384]{2,1,0:T(8,128)(2,1)S(1)}, u32[]{:S(2)}, u32[]{:S(2)}) collective-permute-start(bf16[3,256,384]{2,1,0:T(8,128)(2,1)} %copy-done.12), channel_id=1, source_target_pairs={{0,3},{1,0},{2,1},{3,2},{4,7},{5,4},{6,5},{7,6},{8,11},{9,8},{10,9... | collective-permute-start | bytes 1769480 | tf_op jit(solution)/shard_map/ppermute | solution.py:331
  41.6 8.8 %collective-permute-done.4.before_ref = bf16[2,256,384]{2,1,0:T(8,128)(2,1)S(1)} collective-permute-done((bf16[2,256,384]{2,1,0:T(8,128)(2,1)S(1)}, bf16[2,256,384]{2,1,0:T(8,128)(2,1)S(1)}, u32[]{:S(2)}, u32[]{:S(2)}) %collective-permute-start.4) | collective-permute-done | bytes 393248 | tf_op jit(solution)/shard_map/ppermute | solution.py:331
  50.4 0.1 collective-permute-start.5
  50.5 6.3 %collective-permute-done.5.far_ref = bf16[1,256,384]{2,1,0:T(8,128)(2,1)S(1)} collective-permute-done((bf16[1,256,384]{2,1,0:T(8,128)(2,1)S(1)}, bf16[1,256,384]{2,1,0:T(8,128)(2,1)S(1)}, u32[]{:S(2)}, u32[]{:S(2)}) %collective-permute-start.5) | collective-permute-done | bytes 196640 | tf_op jit(solution)/shard_map/ppermute | solution.py:331
  56.8 0.0 collective-permute-done.3.after_ref
  56.8 5.0 %all-to-all-done = bf16[64,16,384]{2,1,0:T(8,128)(2,1)S(1)} async-done(((bf16[64,16,384]{2,1,0:T(8,128)(2,1)}), bf16[64,16,384]{2,1,0:T(8,128)(2,1)S(1)}, u32[]{:S(2)}, u32[]{:S(2)}) %all-to-all-start) | async-done | bytes 786464 | tf_op jit(solution)/shard_map/all_to_all | solution.py:353
  61.8 0.1 shard_map.88
  61.9 1.2 collective-permute-start.6
  63.0 1.6 %collective-permute-start.8 = (bf16[512,384]{1,0:T(8,128)(2,1)S(1)}, bf16[512,384]{1,0:T(8,128)(2,1)S(1)}, u32[]{:S(2)}, u32[]{:S(2)}) collective-permute-start(bf16[512,384]{1,0:T(8,128)(2,1)S(1)} %get-tuple-element.46.part_ref), channel_id=1, source_target_pairs={{0,3},{1,0},{2,1},{3,2},{4,7},{5,4},{6,5},{7,6},{8,11},{9,8},{10,9... | collective-permute-start | bytes 1179656 | tf_op jit(solution)/shard_map/ppermute | solution.py:331
  64.6 0.0 collective-permute-start.10
  64.6 2.7 %collective-permute-start.11 = (bf16[512,384]{1,0:T(8,128)(2,1)S(1)}, bf16[512,384]{1,0:T(8,128)(2,1)S(1)}, u32[]{:S(2)}, u32[]{:S(2)}) collective-permute-start(bf16[512,384]{1,0:T(8,128)(2,1)S(1)} %get-tuple-element.45.part_ref), channel_id=1, source_target_pairs={{0,3},{1,0},{2,1},{3,2},{4,7},{5,4},{6,5},{7,6},{8,11},{9,8},{10,9... | collective-permute-start | bytes 1179656 | tf_op jit(solution)/shard_map/ppermute | solution.py:331
  67.3 6.2 %collective-permute-done.6.part_ref = bf16[512,384]{1,0:T(8,128)(2,1)S(1)} collective-permute-done((bf16[512,384]{1,0:T(8,128)(2,1)S(1)}, bf16[512,384]{1,0:T(8,128)(2,1)S(1)}, u32[]{:S(2)}, u32[]{:S(2)}) %collective-permute-start.6) | collective-permute-done | bytes 393248 | tf_op jit(solution)/shard_map/ppermute | solution.py:331
  73.5 0.0 collective-permute-start.7
  73.5 0.0 collective-permute-done.8.part_ref
  73.5 2.7 %collective-permute-start.9 = (bf16[512,384]{1,0:T(8,128)(2,1)S(1)}, bf16[512,384]{1,0:T(8,128)(2,1)S(1)}, u32[]{:S(2)}, u32[]{:S(2)}) collective-permute-start(bf16[512,384]{1,0:T(8,128)(2,1)S(1)} %collective-permute-done.8.part_ref), channel_id=1, source_target_pairs={{0,3},{1,0},{2,1},{3,2},{4,7},{5,4},{6,5},{7,6},{8,11},{9,8},{10,9... | collective-permute-start | bytes 1179656 | tf_op jit(solution)/shard_map/ppermute | solution.py:331
  76.1 0.3 shard_map.89.refs_0_.refs_2_.top_ref
  76.4 0.0 copy-start.1
  76.4 0.3 shard_map.90.refs_1_.refs_3_.bottom_ref
  76.7 0.3 shard_map.103.own_square
  77.0 1.4 %shard_map.102 = (bf16[1024,1024]{1,0:T(8,128)(2,1)S(1)}, bf16[1024,1024]{1,0:T(8,128)(2,1)S(1)}) custom-call(s32[1]{0:T(128)} %bitcast.place_ref, f32[256,1024]{1,0:T(8,128)S(1)} %bitcast.10, bf16[3,256,384]{2,1,0:T(8,128)(2,1)S(1)} %collective-permute-done.3.after_ref, bf16[2,256,384]{2,1,0:T(8,128)(2,1)S(1)} %collective-permute-done.4.before_ref, ...), custom_call_target="tpu_custom_call" | custom-call | bytes 16777216 | tf_op jit(solution)/shard_map/pallas_call | solution.py:84
  78.5 0.6 shard_map.100.refs_5_
  79.1 0.3 shard_map.93.refs_2_.refs_0_
  79.3 0.3 shard_map.96.refs_5_.refs_3_
  79.6 2.3 %collective-permute-done.10.part_ref = bf16[512,384]{1,0:T(8,128)(2,1)S(1)} collective-permute-done((bf16[512,384]{1,0:T(8,128)(2,1)S(1)}, bf16[512,384]{1,0:T(8,128)(2,1)S(1)}, u32[]{:S(2)}, u32[]{:S(2)}) %collective-permute-start.10) | collective-permute-done | bytes 393248 | tf_op jit(solution)/shard_map/ppermute | solution.py:331
  81.9 0.3 shard_map.94.refs_3_.refs_1_
  82.1 0.0 collective-permute-done.11.part_ref
  82.1 0.3 shard_map.95.refs_4_.refs_2_
  82.4 0.0 copy-start.2
  82.4 1.0 shard_map.101.value_ref
  83.5 6.8 %collective-permute-done.7.part_ref.top_ref = bf16[512,384]{1,0:T(8,128)(2,1)S(1)} collective-permute-done((bf16[512,384]{1,0:T(8,128)(2,1)S(1)}, bf16[512,384]{1,0:T(8,128)(2,1)S(1)}, u32[]{:S(2)}, u32[]{:S(2)}) %collective-permute-start.7) | collective-permute-done | bytes 393248 | tf_op jit(solution)/shard_map/ppermute | solution.py:331
  90.3 0.0 collective-permute-done.9.part_ref.bottom_ref
  90.3 2.7 %shard_map.104 = (f32[1024,256]{1,0:T(8,128)S(1)}, f32[8,128]{1,0:T(8,128)S(1)}, f32[8,128]{1,0:T(8,128)S(1)}) custom-call(s32[1]{0:T(128)} %bitcast.place_ref, bf16[512,384]{1,0:T(8,128)(2,1)S(1)} %collective-permute-done.7.part_ref.top_ref, bf16[512,384]{1,0:T(8,128)(2,1)S(1)} %collective-permute-done.9.part_ref.bottom_ref, f32[256,1024]{1,0:T(8,128)S(1)} %bitcast.13, ...), custom_call_target="tpu_custom_call" | custom-call | flops 2013265920 | bytes 4194304 | tf_op jit(solution)/shard_map/pallas_call | solution.py:84
  93.1 2.1 %collective-permute-start.12 = (f32[8,128]{1,0:T(8,128)S(1)}, f32[8,128]{1,0:T(8,128)S(1)}, u32[]{:S(2)}, u32[]{:S(2)}) collective-permute-start(f32[8,128]{1,0:T(8,128)S(1)} %get-tuple-element.59.refs_0_), channel_id=1, source_target_pairs={{0,2},{1,3},{2,0},{3,1},{4,6},{5,7},{6,4},{7,5},{8,10},{9,11},{10,... | collective-permute-start | bytes 12296 | tf_op jit(solution)/shard_map/ppermute | solution.py:331
  95.1 0.9 collective-permute-start.13
  96.1 1.7 %collective-permute-start.14 = (f32[8,128]{1,0:T(8,128)S(1)}, f32[8,128]{1,0:T(8,128)S(1)}, u32[]{:S(2)}, u32[]{:S(2)}) collective-permute-start(f32[8,128]{1,0:T(8,128)S(1)} %get-tuple-element.59.refs_0_), channel_id=1, source_target_pairs={{0,3},{1,0},{2,1},{3,2},{4,7},{5,4},{6,5},{7,6},{8,11},{9,8},{10,9... | collective-permute-start | bytes 12296 | tf_op jit(solution)/shard_map/ppermute | solution.py:331
  97.8 1.1 shard_map.105.refs_4_
  98.9 0.2 collective-permute-done.13.refs_2_
  99.1 1.1 shard_map.106
  100.2 8.3 %all-to-all-start.1 = ((bf16[64,40,128]{2,1,0:T(8,128)(2,1)}), bf16[64,40,128]{2,1,0:T(8,128)(2,1)S(1)}, u32[]{:S(2)}, u32[]{:S(2)}) async-start(bf16[64,40,128]{2,1,0:T(8,128)(2,1)} %shard_map.106), calls=%async_computation.1 | async-start | bytes 1310720 | tf_op jit(solution)/shard_map/all_to_all | solution.py:427
  108.5 0.0 copy-start.5
  108.5 1.2 copy-done.5
  109.7 1.2 copy-done.6
  111.0 1.2 shard_map.97
  112.2 0.0 copy-start.8
  112.2 1.9 %shard_map.98 = (f32[256,1024]{1,0:T(8,128)S(1)}, f32[256,1024]{1,0:T(8,128)S(1)}) custom-call(s32[1]{0:T(128)} %bitcast.place_ref, bf16[512,512]{1,0:T(8,128)(2,1)S(1)} %shard_map.89.refs_0_.refs_2_.top_ref, bf16[512,512]{1,0:T(8,128)(2,1)S(1)} %shard_map.90.refs_1_.refs_3_.bottom_ref, bf16[512,512]{1,0:T(8,128)(2,1)S(1)} %shard_map.93.refs_2_.refs_0_, ...), custom_call_target="tpu_custom_call" | custom-call | flops 1610612736 | bytes 4194304 | tf_op jit(solution)/shard_map/pallas_call | solution.py:84
  114.1 0.3 shard_map.91.refs_2_
  114.4 0.3 shard_map.92.refs_3_
  114.6 2.3 %shard_map.99 = (f32[256,1024]{1,0:T(8,128)}, f32[256,1024]{1,0:T(8,128)}) custom-call(s32[1]{0:T(128)} %bitcast.place_ref, bf16[512,512]{1,0:T(8,128)(2,1)S(1)} %shard_map.89.refs_0_.refs_2_.top_ref, bf16[512,512]{1,0:T(8,128)(2,1)S(1)} %shard_map.90.refs_1_.refs_3_.bottom_ref, bf16[512,512]{1,0:T(8,128)(2,1)S(1)} %shard_map.91.refs_2_, ...), custom_call_target="tpu_custom_call" | custom-call | flops 805306368 | bytes 4194304 | tf_op jit(solution)/shard_map/pallas_call | solution.py:84
  117.0 11.7 %all-to-all-done.1.returned_ref = bf16[64,40,128]{2,1,0:T(8,128)(2,1)S(1)} async-done(((bf16[64,40,128]{2,1,0:T(8,128)(2,1)}), bf16[64,40,128]{2,1,0:T(8,128)(2,1)S(1)}, u32[]{:S(2)}, u32[]{:S(2)}) %all-to-all-start.1) | async-done | bytes 655392 | tf_op jit(solution)/shard_map/all_to_all | solution.py:427
  128.6 2.1 %shard_map.107 = f32[48,16,256]{2,1,0:T(8,128)} custom-call(s32[48]{0:T(128)S(1)} %copy-done.11, bf16[64,40,128]{2,1,0:T(8,128)(2,1)S(1)} %all-to-all-done.1.returned_ref), custom_call_target="tpu_custom_call" | custom-call | bytes 4194304 | tf_op jit(solution)/shard_map/pallas_call | solution.py:84
  (20 shorter events, 0.1 us)
Async XLA Ops:
  0.6 8.2 %copy-start = (f32[1,256,1024]{2,1,0:T(8,128)S(1)}, f32[1,256,1024]{2,1,0:T(8,128)}, u32[]{:S(2)}) copy-start(f32[1,256,1024]{2,1,0:T(8,128)} %param.10) | copy-start | bytes 3145732
  0.6 1.5 %copy-start.4 = (bf16[1,48,16,1024]{3,2,1,0:T(8,128)(2,1)S(1)}, bf16[1,48,16,1024]{3,2,1,0:T(8,128)(2,1)}, u32[]{:S(2)}) copy-start(bf16[1,48,16,1024]{3,2,1,0:T(8,128)(2,1)} %param.6) | copy-start | bytes 4718596
  2.1 22.0 %copy-start.11 = (s32[48]{0:T(128)S(1)}, s32[48]{0:T(128)}, u32[]{:S(2)}) copy-start(s32[48]{0:T(128)} %owner_ref.3) | copy-start | bytes 580
  2.3 11.7 %collective-permute-start = (bf16[48,16,256]{2,1,0:T(8,128)(2,1)S(1)}, bf16[48,16,256]{2,1,0:T(8,128)(2,1)S(1)}, u32[]{:S(2)}, u32[]{:S(2)}) collective-permute-start(bf16[48,16,256]{2,1,0:T(8,128)(2,1)S(1)} %get-tuple-element.33), channel_id=1, source_target_pairs={{0,2},{1,3},{2,0},{3,1},{4,6},{5,7},{6,4},{7,5},{8,10},{9,11},{10,... | collective-permute-start | bytes 1179656 | tf_op jit(solution)/shard_map/ppermute | solution.py:331
  6.2 18.0 %collective-permute-start.1 = (bf16[48,16,256]{2,1,0:T(8,128)(2,1)S(1)}, bf16[48,16,256]{2,1,0:T(8,128)(2,1)S(1)}, u32[]{:S(2)}, u32[]{:S(2)}) collective-permute-start(bf16[48,16,256]{2,1,0:T(8,128)(2,1)S(1)} %get-tuple-element.34), channel_id=1, source_target_pairs={{0,1},{1,2},{2,3},{3,0},{4,5},{5,6},{6,7},{7,4},{8,9},{9,10},{10,1... | collective-permute-start | bytes 1179656 | tf_op jit(solution)/shard_map/ppermute | solution.py:331
  6.6 17.6 %collective-permute-start.2 = (bf16[48,16,256]{2,1,0:T(8,128)(2,1)S(1)}, bf16[48,16,256]{2,1,0:T(8,128)(2,1)S(1)}, u32[]{:S(2)}, u32[]{:S(2)}) collective-permute-start(bf16[48,16,256]{2,1,0:T(8,128)(2,1)S(1)} %get-tuple-element.35), channel_id=1, source_target_pairs={{0,3},{1,0},{2,1},{3,2},{4,7},{5,4},{6,5},{7,6},{8,11},{9,8},{10,9... | collective-permute-start | bytes 1179656 | tf_op jit(solution)/shard_map/ppermute | solution.py:331
  9.6 0.8 copy-start.12
  26.4 35.4 %all-to-all-start = ((bf16[64,16,384]{2,1,0:T(8,128)(2,1)}), bf16[64,16,384]{2,1,0:T(8,128)(2,1)S(1)}, u32[]{:S(2)}, u32[]{:S(2)}) async-start(bf16[64,16,384]{2,1,0:T(8,128)(2,1)} %shard_map.87), calls=%async_computation | async-start | bytes 1572864 | tf_op jit(solution)/shard_map/all_to_all | solution.py:353
  38.8 11.5 %collective-permute-start.4 = (bf16[2,256,384]{2,1,0:T(8,128)(2,1)S(1)}, bf16[2,256,384]{2,1,0:T(8,128)(2,1)S(1)}, u32[]{:S(2)}, u32[]{:S(2)}) collective-permute-start(bf16[2,256,384]{2,1,0:T(8,128)(2,1)S(1)} %get-tuple-element.43), channel_id=1, source_target_pairs={{0,1},{1,2},{2,3},{3,0},{4,5},{5,6},{6,7},{7,4},{8,9},{9,10},{10,1... | collective-permute-start | bytes 1179656 | tf_op jit(solution)/shard_map/ppermute | solution.py:331
  40.0 16.8 %collective-permute-start.3 = (bf16[3,256,384]{2,1,0:T(8,128)(2,1)}, bf16[3,256,384]{2,1,0:T(8,128)(2,1)S(1)}, u32[]{:S(2)}, u32[]{:S(2)}) collective-permute-start(bf16[3,256,384]{2,1,0:T(8,128)(2,1)} %copy-done.12), channel_id=1, source_target_pairs={{0,3},{1,0},{2,1},{3,2},{4,7},{5,4},{6,5},{7,6},{8,11},{9,8},{10,9... | collective-permute-start | bytes 1769480 | tf_op jit(solution)/shard_map/ppermute | solution.py:331
  50.4 6.4 %collective-permute-start.5 = (bf16[1,256,384]{2,1,0:T(8,128)(2,1)S(1)}, bf16[1,256,384]{2,1,0:T(8,128)(2,1)S(1)}, u32[]{:S(2)}, u32[]{:S(2)}) collective-permute-start(bf16[1,256,384]{2,1,0:T(8,128)(2,1)S(1)} %slice.4), channel_id=1, source_target_pairs={{0,1},{1,2},{2,3},{3,0},{4,5},{5,6},{6,7},{7,4},{8,9},{9,10},{10,1... | collective-permute-start | bytes 589832 | tf_op jit(solution)/shard_map/ppermute | solution.py:331
  61.9 11.6 %collective-permute-start.6 = (bf16[512,384]{1,0:T(8,128)(2,1)S(1)}, bf16[512,384]{1,0:T(8,128)(2,1)S(1)}, u32[]{:S(2)}, u32[]{:S(2)}) collective-permute-start(bf16[512,384]{1,0:T(8,128)(2,1)S(1)} %get-tuple-element.45.part_ref), channel_id=1, source_target_pairs={{0,1},{1,2},{2,3},{3,0},{4,5},{5,6},{6,7},{7,4},{8,9},{9,10},{10,1... | collective-permute-start | bytes 1179656 | tf_op jit(solution)/shard_map/ppermute | solution.py:331
  63.0 10.4 %collective-permute-start.8 = (bf16[512,384]{1,0:T(8,128)(2,1)S(1)}, bf16[512,384]{1,0:T(8,128)(2,1)S(1)}, u32[]{:S(2)}, u32[]{:S(2)}) collective-permute-start(bf16[512,384]{1,0:T(8,128)(2,1)S(1)} %get-tuple-element.46.part_ref), channel_id=1, source_target_pairs={{0,3},{1,0},{2,1},{3,2},{4,7},{5,4},{6,5},{7,6},{8,11},{9,8},{10,9... | collective-permute-start | bytes 1179656 | tf_op jit(solution)/shard_map/ppermute | solution.py:331
  64.6 17.3 %collective-permute-start.10 = (bf16[512,384]{1,0:T(8,128)(2,1)S(1)}, bf16[512,384]{1,0:T(8,128)(2,1)S(1)}, u32[]{:S(2)}, u32[]{:S(2)}) collective-permute-start(bf16[512,384]{1,0:T(8,128)(2,1)S(1)} %get-tuple-element.46.part_ref), channel_id=1, source_target_pairs={{0,1},{1,2},{2,3},{3,0},{4,5},{5,6},{6,7},{7,4},{8,9},{9,10},{10,1... | collective-permute-start | bytes 1179656 | tf_op jit(solution)/shard_map/ppermute | solution.py:331
  64.6 17.5 %collective-permute-start.11 = (bf16[512,384]{1,0:T(8,128)(2,1)S(1)}, bf16[512,384]{1,0:T(8,128)(2,1)S(1)}, u32[]{:S(2)}, u32[]{:S(2)}) collective-permute-start(bf16[512,384]{1,0:T(8,128)(2,1)S(1)} %get-tuple-element.45.part_ref), channel_id=1, source_target_pairs={{0,3},{1,0},{2,1},{3,2},{4,7},{5,4},{6,5},{7,6},{8,11},{9,8},{10,9... | collective-permute-start | bytes 1179656 | tf_op jit(solution)/shard_map/ppermute | solution.py:331
  73.5 16.9 %collective-permute-start.7 = (bf16[512,384]{1,0:T(8,128)(2,1)S(1)}, bf16[512,384]{1,0:T(8,128)(2,1)S(1)}, u32[]{:S(2)}, u32[]{:S(2)}) collective-permute-start(bf16[512,384]{1,0:T(8,128)(2,1)S(1)} %collective-permute-done.6.part_ref), channel_id=1, source_target_pairs={{0,1},{1,2},{2,3},{3,0},{4,5},{5,6},{6,7},{7,4},{8,9},{9,10},{10,1... | collective-permute-start | bytes 1179656 | tf_op jit(solution)/shard_map/ppermute | solution.py:331
  73.5 16.9 %collective-permute-start.9 = (bf16[512,384]{1,0:T(8,128)(2,1)S(1)}, bf16[512,384]{1,0:T(8,128)(2,1)S(1)}, u32[]{:S(2)}, u32[]{:S(2)}) collective-permute-start(bf16[512,384]{1,0:T(8,128)(2,1)S(1)} %collective-permute-done.8.part_ref), channel_id=1, source_target_pairs={{0,3},{1,0},{2,1},{3,2},{4,7},{5,4},{6,5},{7,6},{8,11},{9,8},{10,9... | collective-permute-start | bytes 1179656 | tf_op jit(solution)/shard_map/ppermute | solution.py:331
  76.4 2.1 %copy-start.1 = (f32[1,256,1024]{2,1,0:T(8,128)S(1)}, f32[1,256,1024]{2,1,0:T(8,128)}, u32[]{:S(2)}) copy-start(f32[1,256,1024]{2,1,0:T(8,128)} %param.11) | copy-start | bytes 3145732
  82.4 1.0 copy-start.2
  90.3 2.7 %copy-start.7 = (bf16[512,384]{1,0:T(8,128)(2,1)}, bf16[512,384]{1,0:T(8,128)(2,1)S(1)}, u32[]{:S(2)}) copy-start(bf16[512,384]{1,0:T(8,128)(2,1)S(1)} %collective-permute-done.7.part_ref.top_ref) | copy-start | bytes 1179652
  90.3 2.7 %copy-start.9 = (bf16[512,384]{1,0:T(8,128)(2,1)}, bf16[512,384]{1,0:T(8,128)(2,1)S(1)}, u32[]{:S(2)}) copy-start(bf16[512,384]{1,0:T(8,128)(2,1)S(1)} %collective-permute-done.9.part_ref.bottom_ref) | copy-start | bytes 1179652
  93.1 5.9 %collective-permute-start.12 = (f32[8,128]{1,0:T(8,128)S(1)}, f32[8,128]{1,0:T(8,128)S(1)}, u32[]{:S(2)}, u32[]{:S(2)}) collective-permute-start(f32[8,128]{1,0:T(8,128)S(1)} %get-tuple-element.59.refs_0_), channel_id=1, source_target_pairs={{0,2},{1,3},{2,0},{3,1},{4,6},{5,7},{6,4},{7,5},{8,10},{9,11},{10,... | collective-permute-start | bytes 12296 | tf_op jit(solution)/shard_map/ppermute | solution.py:331
  95.1 4.0 %collective-permute-start.13 = (f32[8,128]{1,0:T(8,128)S(1)}, f32[8,128]{1,0:T(8,128)S(1)}, u32[]{:S(2)}, u32[]{:S(2)}) collective-permute-start(f32[8,128]{1,0:T(8,128)S(1)} %get-tuple-element.59.refs_0_), channel_id=1, source_target_pairs={{0,1},{1,2},{2,3},{3,0},{4,5},{5,6},{6,7},{7,4},{8,9},{9,10},{10,1... | collective-permute-start | bytes 12296 | tf_op jit(solution)/shard_map/ppermute | solution.py:331
  96.1 3.0 %collective-permute-start.14 = (f32[8,128]{1,0:T(8,128)S(1)}, f32[8,128]{1,0:T(8,128)S(1)}, u32[]{:S(2)}, u32[]{:S(2)}) collective-permute-start(f32[8,128]{1,0:T(8,128)S(1)} %get-tuple-element.59.refs_0_), channel_id=1, source_target_pairs={{0,3},{1,0},{2,1},{3,2},{4,7},{5,4},{6,5},{7,6},{8,11},{9,8},{10,9... | collective-permute-start | bytes 12296 | tf_op jit(solution)/shard_map/ppermute | solution.py:331
  100.2 28.4 %all-to-all-start.1 = ((bf16[64,40,128]{2,1,0:T(8,128)(2,1)}), bf16[64,40,128]{2,1,0:T(8,128)(2,1)S(1)}, u32[]{:S(2)}, u32[]{:S(2)}) async-start(bf16[64,40,128]{2,1,0:T(8,128)(2,1)} %shard_map.106), calls=%async_computation.1 | async-start | bytes 1310720 | tf_op jit(solution)/shard_map/all_to_all | solution.py:427
  108.5 1.2 copy-start.5
  109.7 1.2 copy-start.6
  111.0 1.2 copy-start.3
  112.2 1.9 %copy-start.8 = (bf16[512,384]{1,0:T(8,128)(2,1)S(1)}, bf16[512,384]{1,0:T(8,128)(2,1)}, u32[]{:S(2)}) copy-start(bf16[512,384]{1,0:T(8,128)(2,1)} %copy-done.7) | copy-start | bytes 1179652
  112.2 2.2 %copy-start.10 = (bf16[512,384]{1,0:T(8,128)(2,1)S(1)}, bf16[512,384]{1,0:T(8,128)(2,1)}, u32[]{:S(2)}) copy-start(bf16[512,384]{1,0:T(8,128)(2,1)} %copy-done.9) | copy-start | bytes 1179652

commit v2 on v1

--- a/solution.py
+++ b/solution.py
@@ -76,16 +76,22 @@
     return jax.ShapeDtypeStruct(shape, dtype)
 
 
-def call(kernel, outs, operands, n_smem=0, smem_outs=(), flops=0, cost=4 << 20):
+def call(kernel, outs, operands, n_smem=0, smem_outs=(), flops=0, cost=4 << 20, staged=False):
     several = isinstance(outs, tuple)
     out_specs = tuple(
         SMEM if i in smem_outs else VMEM for i in range(len(outs) if several else 1)
     )
+    scratch = []
+    if staged:
+        out_specs = (pl.BlockSpec(memory_space=pl.ANY),)
+        parts = math.gcd(outs.shape[0], 4)
+        scratch = [pltpu.VMEM(outs.shape, outs.dtype), pltpu.SemaphoreType.DMA((parts,))]
     return pl.pallas_call(
         kernel,
         out_shape=outs,
         in_specs=[SMEM] * n_smem + [VMEM] * (len(operands) - n_smem),
         out_specs=out_specs if several else out_specs[0],
+        scratch_shapes=scratch,
         compiler_params=pltpu.CompilerParams(vmem_limit_bytes=VMEM_LIMIT),
         cost_estimate=pl.CostEstimate(flops=flops, bytes_accessed=cost, transcendentals=0),
     )(*operands)
@@ -283,8 +289,22 @@
             out_ref[o, i * slab : (i + 1) * slab, :] = encode(value * inverse)
 
 
+def in_parts(fill, stage_ref, out_ref, semaphores):
+    parts = semaphores.shape[0]
+    size = stage_ref.shape[0] // parts
+    copies = []
+    for p in range(parts):
+        pl.loop(p * size, (p + 1) * size, unroll=size)(fill)
+        rows = pl.ds(p * size, size)
+        copy = pltpu.make_async_copy(stage_ref.at[rows], out_ref.at[rows], semaphores.at[p])
+        copy.start()
+        copies.append(copy)
+    for copy in copies:
+        copy.wait()
+
+
 def stamp_kernel(peak_ref, *refs):
-    *square_refs, codes_ref, out_ref = refs
+    *square_refs, codes_ref, out_ref, stage_ref, semaphores = refs
     total = square_refs[0][...]
     for ref in square_refs[1:]:
         total = total + ref[...]
@@ -296,24 +316,26 @@
     low = scale - high - middle
     value = jnp.where(row == 0, high, jnp.where(row == 1, middle, jnp.where(row == 2, low, 0.0)))
 
-    @pl.loop(0, out_ref.shape[0], unroll=8)
-    def _(o):
+    def fill(o):
         packet = jnp.concatenate([codes_ref[o].astype(F32), value], axis=0)
-        out_ref[o] = packet.astype(BF16)
-
-
-def reorder_kernel(owner_ref, returned_ref, out_ref):
+        stage_ref[o] = packet.astype(BF16)
+
+    in_parts(fill, stage_ref, out_ref, semaphores)
+
+
+def reorder_kernel(owner_ref, returned_ref, out_ref, stage_ref, semaphores):
     slab = out_ref.shape[1]
     lanes = returned_ref.shape[2]
     pieces = out_ref.shape[2] // lanes
 
-    @pl.loop(0, out_ref.shape[0], unroll=16)
-    def _(b):
+    def fill(b):
         packet = returned_ref[owner_ref[b]].astype(F32)
         scale = jnp.sum(packet[pieces * slab :], axis=0, keepdims=True)
         for i in range(pieces):
             value = decode(packet[i * slab : (i + 1) * slab])
-            out_ref[b, :, i * lanes : (i + 1) * lanes] = value * scale
+            stage_ref[b, :, i * lanes : (i + 1) * lanes] = value * scale
+
+    in_parts(fill, stage_ref, out_ref, semaphores)
 
 
 def per_device(grad_parts, block_owner, left_stat, right_stat, root_left, root_right):
@@ -423,7 +445,7 @@
         [result, peak],
         cost=16 << 20,
     )
-    codes = call(stamp_kernel, like((owners, part * slab // 128 + 8, 128), BF16), [peak, *squares, codes])
+    codes = call(stamp_kernel, like((owners, part * slab // 128 + 8, 128), BF16), [peak, *squares, codes], staged=True)
     returned = lax.all_to_all(codes, "fsdp", split_axis=0, concat_axis=0, tiled=True)
     left, right = call(
         functools.partial(statistics_kernel, scale, (2,), False),
@@ -433,7 +455,7 @@
         flops=2 * macs,
     )
     direction = call(
-        reorder_kernel, like((blocks, slab, part)), [block_owner, returned], 1
+        reorder_kernel, like((blocks, slab, part)), [block_owner, returned], 1, staged=True
     )
     return (left[None], right[None], direction)
 

time: 131 us -> 131 us (level)
  no operation moved by 1% of the time
where the time goes in v2:
time: 131 us
  waiting for transfers between devices  61 us (47%)
  starting transfers between devices  42.9 us (33%)
  Pallas kernels  20.8 us (16%)
  local copies, waits for them, and re-layouts  4.8 us (4%)
    ppermute x15, waiting for transfers between devices, shifted(): lax.ppermute(value, 'dp', [(i, (i + k) % replicas) for i in range(replica...  44.3 us
    ppermute x15, starting transfers between devices, shifted(): lax.ppermute(value, 'dp', [(i, (i + k) % replicas) for i in range(replica...  22.2 us
    pallas_call x23, Pallas kernels, call(): pl.pallas_call(kernel, out_shape=outs, in_specs=[SMEM] * n_smem + [VMEM]...  20.8 us
    all_to_all x1, starting transfers between devices, per_device(): lax.all_to_all(outgoing, 'fsdp', split_axis=0, concat_axis=0, tiled=True)  12.4 us
    all_to_all x1, waiting for transfers between devices, per_device(): lax.all_to_all(codes, 'fsdp', split_axis=0, concat_axis=0, tiled=True)  11.7 us
    all_to_all x1, starting transfers between devices, per_device(): lax.all_to_all(codes, 'fsdp', split_axis=0, concat_axis=0, tiled=True)  8.31 us
    all_to_all x1, waiting for transfers between devices, per_device(): lax.all_to_all(outgoing, 'fsdp', split_axis=0, concat_axis=0, tiled=True)  5.04 us
    unnamed x26, local copies, waits for them, and re-layouts  4.78 us
  transfers between devices with their start and end apart: 17, of which 10 were waited for; matrix products, arithmetic and copies ran while one was open for 0% of the time, Pallas kernels for 10%

profile of v2, /device:TPU:1, one launch (start us, length us, event | category | flops | bytes accessed | tf_op | source)
XLA Modules:
  0.0 130.7 jit_solution(3786545543549367599)
XLA Ops:
  0.7 1.5 %copy-done.4 = bf16[1,48,16,1024]{3,2,1,0:T(8,128)(2,1)S(1)} copy-done((bf16[1,48,16,1024]{3,2,1,0:T(8,128)(2,1)S(1)}, bf16[1,48,16,1024]{3,2,1,0:T(8,128)(2,1)}, u32[]{:S(2)}) %copy-start.4) | copy-done | bytes 1572888
  2.1 0.2 shard_map.85
  2.3 3.8 %collective-permute-start = (bf16[48,16,256]{2,1,0:T(8,128)(2,1)S(1)}, bf16[48,16,256]{2,1,0:T(8,128)(2,1)S(1)}, u32[]{:S(2)}, u32[]{:S(2)}) collective-permute-start(bf16[48,16,256]{2,1,0:T(8,128)(2,1)S(1)} %get-tuple-element.33), channel_id=1, source_target_pairs={{0,2},{1,3},{2,0},{3,1},{4,6},{5,7},{6,4},{7,5},{8,10},{9,11},{10,... | collective-permute-start | bytes 1179656 | tf_op jit(solution)/shard_map/ppermute | solution.py:353
  6.2 0.4 collective-permute-start.1
  6.6 2.3 %collective-permute-start.2 = (bf16[48,16,256]{2,1,0:T(8,128)(2,1)S(1)}, bf16[48,16,256]{2,1,0:T(8,128)(2,1)S(1)}, u32[]{:S(2)}, u32[]{:S(2)}) collective-permute-start(bf16[48,16,256]{2,1,0:T(8,128)(2,1)S(1)} %get-tuple-element.35), channel_id=1, source_target_pairs={{0,3},{1,0},{2,1},{3,2},{4,7},{5,4},{6,5},{7,6},{8,11},{9,8},{10,9... | collective-permute-start | bytes 1179656 | tf_op jit(solution)/shard_map/ppermute | solution.py:353
  8.9 0.8 shard_map.86
  9.6 0.0 copy-start.12
  9.6 0.8 copy-done.12
  10.4 3.6 %collective-permute-done.refs_1_ = bf16[48,16,256]{2,1,0:T(8,128)(2,1)S(1)} collective-permute-done((bf16[48,16,256]{2,1,0:T(8,128)(2,1)S(1)}, bf16[48,16,256]{2,1,0:T(8,128)(2,1)S(1)}, u32[]{:S(2)}, u32[]{:S(2)}) %collective-permute-start) | collective-permute-done | bytes 393248 | tf_op jit(solution)/shard_map/ppermute | solution.py:353
  14.1 10.1 %collective-permute-done.1.refs_2_ = bf16[48,16,256]{2,1,0:T(8,128)(2,1)S(1)} collective-permute-done((bf16[48,16,256]{2,1,0:T(8,128)(2,1)S(1)}, bf16[48,16,256]{2,1,0:T(8,128)(2,1)S(1)}, u32[]{:S(2)}, u32[]{:S(2)}) %collective-permute-start.1) | collective-permute-done | bytes 393248 | tf_op jit(solution)/shard_map/ppermute | solution.py:353
  24.2 0.0 collective-permute-done.2.refs_3_
  24.2 2.2 %shard_map.87 = bf16[64,16,384]{2,1,0:T(8,128)(2,1)} custom-call(s32[48]{0:T(128)S(1)} %copy-done.11, bf16[48,16,256]{2,1,0:T(8,128)(2,1)S(1)} %get-tuple-element.38.refs_0_, bf16[48,16,256]{2,1,0:T(8,128)(2,1)S(1)} %collective-permute-done.refs_1_, bf16[48,16,256]{2,1,0:T(8,128)(2,1)S(1)} %collective-permute-done.1.refs_2_, ...), custom_call_target="tpu_custom_call" | custom-call | bytes 4194304 | tf_op jit(solution)/shard_map/pallas_call | solution.py:89
  26.4 12.4 %all-to-all-start = ((bf16[64,16,384]{2,1,0:T(8,128)(2,1)}), bf16[64,16,384]{2,1,0:T(8,128)(2,1)S(1)}, u32[]{:S(2)}, u32[]{:S(2)}) async-start(bf16[64,16,384]{2,1,0:T(8,128)(2,1)} %shard_map.87), calls=%async_computation | async-start | bytes 1572864 | tf_op jit(solution)/shard_map/all_to_all | solution.py:375
  38.8 1.2 collective-permute-start.4
  40.0 1.6 %collective-permute-start.3 = (bf16[3,256,384]{2,1,0:T(8,128)(2,1)}, bf16[3,256,384]{2,1,0:T(8,128)(2,1)S(1)}, u32[]{:S(2)}, u32[]{:S(2)}) collective-permute-start(bf16[3,256,384]{2,1,0:T(8,128)(2,1)} %copy-done.12), channel_id=1, source_target_pairs={{0,3},{1,0},{2,1},{3,2},{4,7},{5,4},{6,5},{7,6},{8,11},{9,8},{10,9... | collective-permute-start | bytes 1769480 | tf_op jit(solution)/shard_map/ppermute | solution.py:353
  41.6 8.8 %collective-permute-done.4.before_ref = bf16[2,256,384]{2,1,0:T(8,128)(2,1)S(1)} collective-permute-done((bf16[2,256,384]{2,1,0:T(8,128)(2,1)S(1)}, bf16[2,256,384]{2,1,0:T(8,128)(2,1)S(1)}, u32[]{:S(2)}, u32[]{:S(2)}) %collective-permute-start.4) | collective-permute-done | bytes 393248 | tf_op jit(solution)/shard_map/ppermute | solution.py:353
  50.4 0.1 collective-permute-start.5
  50.5 6.3 %collective-permute-done.5.far_ref = bf16[1,256,384]{2,1,0:T(8,128)(2,1)S(1)} collective-permute-done((bf16[1,256,384]{2,1,0:T(8,128)(2,1)S(1)}, bf16[1,256,384]{2,1,0:T(8,128)(2,1)S(1)}, u32[]{:S(2)}, u32[]{:S(2)}) %collective-permute-start.5) | collective-permute-done | bytes 196640 | tf_op jit(solution)/shard_map/ppermute | solution.py:353
  56.8 0.0 collective-permute-done.3.after_ref
  56.8 5.0 %all-to-all-done = bf16[64,16,384]{2,1,0:T(8,128)(2,1)S(1)} async-done(((bf16[64,16,384]{2,1,0:T(8,128)(2,1)}), bf16[64,16,384]{2,1,0:T(8,128)(2,1)S(1)}, u32[]{:S(2)}, u32[]{:S(2)}) %all-to-all-start) | async-done | bytes 786464 | tf_op jit(solution)/shard_map/all_to_all | solution.py:375
  61.8 0.1 shard_map.88
  61.9 1.2 collective-permute-start.6
  63.0 1.6 %collective-permute-start.8 = (bf16[512,384]{1,0:T(8,128)(2,1)S(1)}, bf16[512,384]{1,0:T(8,128)(2,1)S(1)}, u32[]{:S(2)}, u32[]{:S(2)}) collective-permute-start(bf16[512,384]{1,0:T(8,128)(2,1)S(1)} %get-tuple-element.46.part_ref), channel_id=1, source_target_pairs={{0,3},{1,0},{2,1},{3,2},{4,7},{5,4},{6,5},{7,6},{8,11},{9,8},{10,9... | collective-permute-start | bytes 1179656 | tf_op jit(solution)/shard_map/ppermute | solution.py:353
  64.6 0.0 collective-permute-start.10
  64.6 2.7 %collective-permute-start.11 = (bf16[512,384]{1,0:T(8,128)(2,1)S(1)}, bf16[512,384]{1,0:T(8,128)(2,1)S(1)}, u32[]{:S(2)}, u32[]{:S(2)}) collective-permute-start(bf16[512,384]{1,0:T(8,128)(2,1)S(1)} %get-tuple-element.45.part_ref), channel_id=1, source_target_pairs={{0,3},{1,0},{2,1},{3,2},{4,7},{5,4},{6,5},{7,6},{8,11},{9,8},{10,9... | collective-permute-start | bytes 1179656 | tf_op jit(solution)/shard_map/ppermute | solution.py:353
  67.3 6.2 %collective-permute-done.6.part_ref = bf16[512,384]{1,0:T(8,128)(2,1)S(1)} collective-permute-done((bf16[512,384]{1,0:T(8,128)(2,1)S(1)}, bf16[512,384]{1,0:T(8,128)(2,1)S(1)}, u32[]{:S(2)}, u32[]{:S(2)}) %collective-permute-start.6) | collective-permute-done | bytes 393248 | tf_op jit(solution)/shard_map/ppermute | solution.py:353
  73.5 0.0 collective-permute-start.7
  73.5 0.0 collective-permute-done.8.part_ref
  73.5 2.7 %collective-permute-start.9 = (bf16[512,384]{1,0:T(8,128)(2,1)S(1)}, bf16[512,384]{1,0:T(8,128)(2,1)S(1)}, u32[]{:S(2)}, u32[]{:S(2)}) collective-permute-start(bf16[512,384]{1,0:T(8,128)(2,1)S(1)} %collective-permute-done.8.part_ref), channel_id=1, source_target_pairs={{0,3},{1,0},{2,1},{3,2},{4,7},{5,4},{6,5},{7,6},{8,11},{9,8},{10,9... | collective-permute-start | bytes 1179656 | tf_op jit(solution)/shard_map/ppermute | solution.py:353
  76.1 0.3 shard_map.89.refs_0_.refs_2_.top_ref
  76.4 0.0 copy-start.1
  76.4 0.3 shard_map.90.refs_1_.refs_3_.bottom_ref
  76.7 0.3 shard_map.103.own_square
  77.0 1.4 %shard_map.102 = (bf16[1024,1024]{1,0:T(8,128)(2,1)S(1)}, bf16[1024,1024]{1,0:T(8,128)(2,1)S(1)}) custom-call(s32[1]{0:T(128)} %bitcast.place_ref, f32[256,1024]{1,0:T(8,128)S(1)} %bitcast.10, bf16[3,256,384]{2,1,0:T(8,128)(2,1)S(1)} %collective-permute-done.3.after_ref, bf16[2,256,384]{2,1,0:T(8,128)(2,1)S(1)} %collective-permute-done.4.before_ref, ...), custom_call_target="tpu_custom_call" | custom-call | bytes 16777216 | tf_op jit(solution)/shard_map/pallas_call | solution.py:89
  78.5 0.6 shard_map.100.refs_5_
  79.1 0.3 shard_map.93.refs_2_.refs_0_
  79.3 0.3 shard_map.96.refs_5_.refs_3_
  79.6 2.3 %collective-permute-done.10.part_ref = bf16[512,384]{1,0:T(8,128)(2,1)S(1)} collective-permute-done((bf16[512,384]{1,0:T(8,128)(2,1)S(1)}, bf16[512,384]{1,0:T(8,128)(2,1)S(1)}, u32[]{:S(2)}, u32[]{:S(2)}) %collective-permute-start.10) | collective-permute-done | bytes 393248 | tf_op jit(solution)/shard_map/ppermute | solution.py:353
  81.9 0.3 shard_map.94.refs_3_.refs_1_
  82.1 0.0 collective-permute-done.11.part_ref
  82.1 0.3 shard_map.95.refs_4_.refs_2_
  82.4 0.0 copy-start.2
  82.4 1.0 shard_map.101.value_ref
  83.5 6.8 %collective-permute-done.7.part_ref.top_ref = bf16[512,384]{1,0:T(8,128)(2,1)S(1)} collective-permute-done((bf16[512,384]{1,0:T(8,128)(2,1)S(1)}, bf16[512,384]{1,0:T(8,128)(2,1)S(1)}, u32[]{:S(2)}, u32[]{:S(2)}) %collective-permute-start.7) | collective-permute-done | bytes 393248 | tf_op jit(solution)/shard_map/ppermute | solution.py:353
  90.3 2.7 %shard_map.104 = (f32[1024,256]{1,0:T(8,128)S(1)}, f32[8,128]{1,0:T(8,128)S(1)}, f32[8,128]{1,0:T(8,128)S(1)}) custom-call(s32[1]{0:T(128)} %bitcast.place_ref, bf16[512,384]{1,0:T(8,128)(2,1)S(1)} %collective-permute-done.7.part_ref.top_ref, bf16[512,384]{1,0:T(8,128)(2,1)S(1)} %collective-permute-done.9.part_ref.bottom_ref, f32[256,1024]{1,0:T(8,128)S(1)} %bitcast.13, ...), custom_call_target="tpu_custom_call" | custom-call | flops 2013265920 | bytes 4194304 | tf_op jit(solution)/shard_map/pallas_call | solution.py:89
  93.1 2.1 %collective-permute-start.12 = (f32[8,128]{1,0:T(8,128)S(1)}, f32[8,128]{1,0:T(8,128)S(1)}, u32[]{:S(2)}, u32[]{:S(2)}) collective-permute-start(f32[8,128]{1,0:T(8,128)S(1)} %get-tuple-element.59.refs_0_), channel_id=1, source_target_pairs={{0,2},{1,3},{2,0},{3,1},{4,6},{5,7},{6,4},{7,5},{8,10},{9,11},{10,... | collective-permute-start | bytes 12296 | tf_op jit(solution)/shard_map/ppermute | solution.py:353
  95.1 0.9 collective-permute-start.13
  96.1 1.7 %collective-permute-start.14 = (f32[8,128]{1,0:T(8,128)S(1)}, f32[8,128]{1,0:T(8,128)S(1)}, u32[]{:S(2)}, u32[]{:S(2)}) collective-permute-start(f32[8,128]{1,0:T(8,128)S(1)} %get-tuple-element.59.refs_0_), channel_id=1, source_target_pairs={{0,3},{1,0},{2,1},{3,2},{4,7},{5,4},{6,5},{7,6},{8,11},{9,8},{10,9... | collective-permute-start | bytes 12296 | tf_op jit(solution)/shard_map/ppermute | solution.py:353
  97.8 1.1 shard_map.105.refs_4_
  98.9 0.0 collective-permute-done.12.refs_1_
  98.9 0.2 collective-permute-done.13.refs_2_
  99.1 1.0 shard_map.106
  100.1 8.3 %all-to-all-start.1 = ((bf16[64,40,128]{2,1,0:T(8,128)(2,1)}), bf16[64,40,128]{2,1,0:T(8,128)(2,1)S(1)}, u32[]{:S(2)}, u32[]{:S(2)}) async-start(bf16[64,40,128]{2,1,0:T(8,128)(2,1)} %shard_map.106), calls=%async_computation.1 | async-start | bytes 1310720 | tf_op jit(solution)/shard_map/all_to_all | solution.py:449
  108.5 0.0 copy-start.5
  108.5 1.2 copy-done.5
  109.7 1.2 copy-done.6
  110.9 1.2 shard_map.97
  112.1 0.0 copy-start.8
  112.1 1.9 %shard_map.98 = (f32[256,1024]{1,0:T(8,128)S(1)}, f32[256,1024]{1,0:T(8,128)S(1)}) custom-call(s32[1]{0:T(128)} %bitcast.place_ref, bf16[512,512]{1,0:T(8,128)(2,1)S(1)} %shard_map.89.refs_0_.refs_2_.top_ref, bf16[512,512]{1,0:T(8,128)(2,1)S(1)} %shard_map.90.refs_1_.refs_3_.bottom_ref, bf16[512,512]{1,0:T(8,128)(2,1)S(1)} %shard_map.93.refs_2_.refs_0_, ...), custom_call_target="tpu_custom_call" | custom-call | flops 1610612736 | bytes 4194304 | tf_op jit(solution)/shard_map/pallas_call | solution.py:89
  114.0 0.3 shard_map.91.refs_2_
  114.3 0.3 shard_map.92.refs_3_
  114.6 2.3 %shard_map.99 = (f32[256,1024]{1,0:T(8,128)}, f32[256,1024]{1,0:T(8,128)}) custom-call(s32[1]{0:T(128)} %bitcast.place_ref, bf16[512,512]{1,0:T(8,128)(2,1)S(1)} %shard_map.89.refs_0_.refs_2_.top_ref, bf16[512,512]{1,0:T(8,128)(2,1)S(1)} %shard_map.90.refs_1_.refs_3_.bottom_ref, bf16[512,512]{1,0:T(8,128)(2,1)S(1)} %shard_map.91.refs_2_, ...), custom_call_target="tpu_custom_call" | custom-call | flops 805306368 | bytes 4194304 | tf_op jit(solution)/shard_map/pallas_call | solution.py:89
  116.9 11.7 %all-to-all-done.1.returned_ref = bf16[64,40,128]{2,1,0:T(8,128)(2,1)S(1)} async-done(((bf16[64,40,128]{2,1,0:T(8,128)(2,1)}), bf16[64,40,128]{2,1,0:T(8,128)(2,1)S(1)}, u32[]{:S(2)}, u32[]{:S(2)}) %all-to-all-start.1) | async-done | bytes 655392 | tf_op jit(solution)/shard_map/all_to_all | solution.py:449
  128.6 1.9 %shard_map.107 = f32[48,16,256]{2,1,0:T(8,128)} custom-call(s32[48]{0:T(128)S(1)} %copy-done.11, bf16[64,40,128]{2,1,0:T(8,128)(2,1)S(1)} %all-to-all-done.1.returned_ref), custom_call_target="tpu_custom_call" | custom-call | bytes 4194304 | tf_op jit(solution)/shard_map/pallas_call | solution.py:89
  (20 shorter events, 0.1 us)
Async XLA Ops:
  0.6 8.2 %copy-start = (f32[1,256,1024]{2,1,0:T(8,128)S(1)}, f32[1,256,1024]{2,1,0:T(8,128)}, u32[]{:S(2)}) copy-start(f32[1,256,1024]{2,1,0:T(8,128)} %param.10) | copy-start | bytes 3145732
  0.6 1.5 %copy-start.4 = (bf16[1,48,16,1024]{3,2,1,0:T(8,128)(2,1)S(1)}, bf16[1,48,16,1024]{3,2,1,0:T(8,128)(2,1)}, u32[]{:S(2)}) copy-start(bf16[1,48,16,1024]{3,2,1,0:T(8,128)(2,1)} %param.6) | copy-start | bytes 4718596
  2.1 22.0 %copy-start.11 = (s32[48]{0:T(128)S(1)}, s32[48]{0:T(128)}, u32[]{:S(2)}) copy-start(s32[48]{0:T(128)} %owner_ref.3) | copy-start | bytes 580
  2.3 11.7 %collective-permute-start = (bf16[48,16,256]{2,1,0:T(8,128)(2,1)S(1)}, bf16[48,16,256]{2,1,0:T(8,128)(2,1)S(1)}, u32[]{:S(2)}, u32[]{:S(2)}) collective-permute-start(bf16[48,16,256]{2,1,0:T(8,128)(2,1)S(1)} %get-tuple-element.33), channel_id=1, source_target_pairs={{0,2},{1,3},{2,0},{3,1},{4,6},{5,7},{6,4},{7,5},{8,10},{9,11},{10,... | collective-permute-start | bytes 1179656 | tf_op jit(solution)/shard_map/ppermute | solution.py:353
  6.2 18.0 %collective-permute-start.1 = (bf16[48,16,256]{2,1,0:T(8,128)(2,1)S(1)}, bf16[48,16,256]{2,1,0:T(8,128)(2,1)S(1)}, u32[]{:S(2)}, u32[]{:S(2)}) collective-permute-start(bf16[48,16,256]{2,1,0:T(8,128)(2,1)S(1)} %get-tuple-element.34), channel_id=1, source_target_pairs={{0,1},{1,2},{2,3},{3,0},{4,5},{5,6},{6,7},{7,4},{8,9},{9,10},{10,1... | collective-permute-start | bytes 1179656 | tf_op jit(solution)/shard_map/ppermute | solution.py:353
  6.6 17.6 %collective-permute-start.2 = (bf16[48,16,256]{2,1,0:T(8,128)(2,1)S(1)}, bf16[48,16,256]{2,1,0:T(8,128)(2,1)S(1)}, u32[]{:S(2)}, u32[]{:S(2)}) collective-permute-start(bf16[48,16,256]{2,1,0:T(8,128)(2,1)S(1)} %get-tuple-element.35), channel_id=1, source_target_pairs={{0,3},{1,0},{2,1},{3,2},{4,7},{5,4},{6,5},{7,6},{8,11},{9,8},{10,9... | collective-permute-start | bytes 1179656 | tf_op jit(solution)/shard_map/ppermute | solution.py:353
  9.6 0.8 copy-start.12
  26.4 35.4 %all-to-all-start = ((bf16[64,16,384]{2,1,0:T(8,128)(2,1)}), bf16[64,16,384]{2,1,0:T(8,128)(2,1)S(1)}, u32[]{:S(2)}, u32[]{:S(2)}) async-start(bf16[64,16,384]{2,1,0:T(8,128)(2,1)} %shard_map.87), calls=%async_computation | async-start | bytes 1572864 | tf_op jit(solution)/shard_map/all_to_all | solution.py:375
  38.8 11.5 %collective-permute-start.4 = (bf16[2,256,384]{2,1,0:T(8,128)(2,1)S(1)}, bf16[2,256,384]{2,1,0:T(8,128)(2,1)S(1)}, u32[]{:S(2)}, u32[]{:S(2)}) collective-permute-start(bf16[2,256,384]{2,1,0:T(8,128)(2,1)S(1)} %get-tuple-element.43), channel_id=1, source_target_pairs={{0,1},{1,2},{2,3},{3,0},{4,5},{5,6},{6,7},{7,4},{8,9},{9,10},{10,1... | collective-permute-start | bytes 1179656 | tf_op jit(solution)/shard_map/ppermute | solution.py:353
  40.0 16.8 %collective-permute-start.3 = (bf16[3,256,384]{2,1,0:T(8,128)(2,1)}, bf16[3,256,384]{2,1,0:T(8,128)(2,1)S(1)}, u32[]{:S(2)}, u32[]{:S(2)}) collective-permute-start(bf16[3,256,384]{2,1,0:T(8,128)(2,1)} %copy-done.12), channel_id=1, source_target_pairs={{0,3},{1,0},{2,1},{3,2},{4,7},{5,4},{6,5},{7,6},{8,11},{9,8},{10,9... | collective-permute-start | bytes 1769480 | tf_op jit(solution)/shard_map/ppermute | solution.py:353
  50.4 6.4 %collective-permute-start.5 = (bf16[1,256,384]{2,1,0:T(8,128)(2,1)S(1)}, bf16[1,256,384]{2,1,0:T(8,128)(2,1)S(1)}, u32[]{:S(2)}, u32[]{:S(2)}) collective-permute-start(bf16[1,256,384]{2,1,0:T(8,128)(2,1)S(1)} %slice.4), channel_id=1, source_target_pairs={{0,1},{1,2},{2,3},{3,0},{4,5},{5,6},{6,7},{7,4},{8,9},{9,10},{10,1... | collective-permute-start | bytes 589832 | tf_op jit(solution)/shard_map/ppermute | solution.py:353
  61.9 11.6 %collective-permute-start.6 = (bf16[512,384]{1,0:T(8,128)(2,1)S(1)}, bf16[512,384]{1,0:T(8,128)(2,1)S(1)}, u32[]{:S(2)}, u32[]{:S(2)}) collective-permute-start(bf16[512,384]{1,0:T(8,128)(2,1)S(1)} %get-tuple-element.45.part_ref), channel_id=1, source_target_pairs={{0,1},{1,2},{2,3},{3,0},{4,5},{5,6},{6,7},{7,4},{8,9},{9,10},{10,1... | collective-permute-start | bytes 1179656 | tf_op jit(solution)/shard_map/ppermute | solution.py:353
  63.0 10.4 %collective-permute-start.8 = (bf16[512,384]{1,0:T(8,128)(2,1)S(1)}, bf16[512,384]{1,0:T(8,128)(2,1)S(1)}, u32[]{:S(2)}, u32[]{:S(2)}) collective-permute-start(bf16[512,384]{1,0:T(8,128)(2,1)S(1)} %get-tuple-element.46.part_ref), channel_id=1, source_target_pairs={{0,3},{1,0},{2,1},{3,2},{4,7},{5,4},{6,5},{7,6},{8,11},{9,8},{10,9... | collective-permute-start | bytes 1179656 | tf_op jit(solution)/shard_map/ppermute | solution.py:353
  64.6 17.3 %collective-permute-start.10 = (bf16[512,384]{1,0:T(8,128)(2,1)S(1)}, bf16[512,384]{1,0:T(8,128)(2,1)S(1)}, u32[]{:S(2)}, u32[]{:S(2)}) collective-permute-start(bf16[512,384]{1,0:T(8,128)(2,1)S(1)} %get-tuple-element.46.part_ref), channel_id=1, source_target_pairs={{0,1},{1,2},{2,3},{3,0},{4,5},{5,6},{6,7},{7,4},{8,9},{9,10},{10,1... | collective-permute-start | bytes 1179656 | tf_op jit(solution)/shard_map/ppermute | solution.py:353
  64.6 17.5 %collective-permute-start.11 = (bf16[512,384]{1,0:T(8,128)(2,1)S(1)}, bf16[512,384]{1,0:T(8,128)(2,1)S(1)}, u32[]{:S(2)}, u32[]{:S(2)}) collective-permute-start(bf16[512,384]{1,0:T(8,128)(2,1)S(1)} %get-tuple-element.45.part_ref), channel_id=1, source_target_pairs={{0,3},{1,0},{2,1},{3,2},{4,7},{5,4},{6,5},{7,6},{8,11},{9,8},{10,9... | collective-permute-start | bytes 1179656 | tf_op jit(solution)/shard_map/ppermute | solution.py:353
  73.5 16.9 %collective-permute-start.7 = (bf16[512,384]{1,0:T(8,128)(2,1)S(1)}, bf16[512,384]{1,0:T(8,128)(2,1)S(1)}, u32[]{:S(2)}, u32[]{:S(2)}) collective-permute-start(bf16[512,384]{1,0:T(8,128)(2,1)S(1)} %collective-permute-done.6.part_ref), channel_id=1, source_target_pairs={{0,1},{1,2},{2,3},{3,0},{4,5},{5,6},{6,7},{7,4},{8,9},{9,10},{10,1... | collective-permute-start | bytes 1179656 | tf_op jit(solution)/shard_map/ppermute | solution.py:353
  73.5 16.9 %collective-permute-start.9 = (bf16[512,384]{1,0:T(8,128)(2,1)S(1)}, bf16[512,384]{1,0:T(8,128)(2,1)S(1)}, u32[]{:S(2)}, u32[]{:S(2)}) collective-permute-start(bf16[512,384]{1,0:T(8,128)(2,1)S(1)} %collective-permute-done.8.part_ref), channel_id=1, source_target_pairs={{0,3},{1,0},{2,1},{3,2},{4,7},{5,4},{6,5},{7,6},{8,11},{9,8},{10,9... | collective-permute-start | bytes 1179656 | tf_op jit(solution)/shard_map/ppermute | solution.py:353
  76.4 2.1 %copy-start.1 = (f32[1,256,1024]{2,1,0:T(8,128)S(1)}, f32[1,256,1024]{2,1,0:T(8,128)}, u32[]{:S(2)}) copy-start(f32[1,256,1024]{2,1,0:T(8,128)} %param.11) | copy-start | bytes 3145732
  82.4 1.0 copy-start.2
  90.3 2.7 %copy-start.7 = (bf16[512,384]{1,0:T(8,128)(2,1)}, bf16[512,384]{1,0:T(8,128)(2,1)S(1)}, u32[]{:S(2)}) copy-start(bf16[512,384]{1,0:T(8,128)(2,1)S(1)} %collective-permute-done.7.part_ref.top_ref) | copy-start | bytes 1179652
  90.3 2.7 %copy-start.9 = (bf16[512,384]{1,0:T(8,128)(2,1)}, bf16[512,384]{1,0:T(8,128)(2,1)S(1)}, u32[]{:S(2)}) copy-start(bf16[512,384]{1,0:T(8,128)(2,1)S(1)} %collective-permute-done.9.part_ref.bottom_ref) | copy-start | bytes 1179652
  93.1 5.9 %collective-permute-start.12 = (f32[8,128]{1,0:T(8,128)S(1)}, f32[8,128]{1,0:T(8,128)S(1)}, u32[]{:S(2)}, u32[]{:S(2)}) collective-permute-start(f32[8,128]{1,0:T(8,128)S(1)} %get-tuple-element.59.refs_0_), channel_id=1, source_target_pairs={{0,2},{1,3},{2,0},{3,1},{4,6},{5,7},{6,4},{7,5},{8,10},{9,11},{10,... | collective-permute-start | bytes 12296 | tf_op jit(solution)/shard_map/ppermute | solution.py:353
  95.1 4.0 %collective-permute-start.13 = (f32[8,128]{1,0:T(8,128)S(1)}, f32[8,128]{1,0:T(8,128)S(1)}, u32[]{:S(2)}, u32[]{:S(2)}) collective-permute-start(f32[8,128]{1,0:T(8,128)S(1)} %get-tuple-element.59.refs_0_), channel_id=1, source_target_pairs={{0,1},{1,2},{2,3},{3,0},{4,5},{5,6},{6,7},{7,4},{8,9},{9,10},{10,1... | collective-permute-start | bytes 12296 | tf_op jit(solution)/shard_map/ppermute | solution.py:353
  96.1 3.0 %collective-permute-start.14 = (f32[8,128]{1,0:T(8,128)S(1)}, f32[8,128]{1,0:T(8,128)S(1)}, u32[]{:S(2)}, u32[]{:S(2)}) collective-permute-start(f32[8,128]{1,0:T(8,128)S(1)} %get-tuple-element.59.refs_0_), channel_id=1, source_target_pairs={{0,3},{1,0},{2,1},{3,2},{4,7},{5,4},{6,5},{7,6},{8,11},{9,8},{10,9... | collective-permute-start | bytes 12296 | tf_op jit(solution)/shard_map/ppermute | solution.py:353
  100.1 28.4 %all-to-all-start.1 = ((bf16[64,40,128]{2,1,0:T(8,128)(2,1)}), bf16[64,40,128]{2,1,0:T(8,128)(2,1)S(1)}, u32[]{:S(2)}, u32[]{:S(2)}) async-start(bf16[64,40,128]{2,1,0:T(8,128)(2,1)} %shard_map.106), calls=%async_computation.1 | async-start | bytes 1310720 | tf_op jit(solution)/shard_map/all_to_all | solution.py:449
  108.5 1.2 copy-start.5
  109.7 1.2 copy-start.6
  110.9 1.2 copy-start.3
  112.1 1.9 %copy-start.8 = (bf16[512,384]{1,0:T(8,128)(2,1)S(1)}, bf16[512,384]{1,0:T(8,128)(2,1)}, u32[]{:S(2)}) copy-start(bf16[512,384]{1,0:T(8,128)(2,1)} %copy-done.7) | copy-start | bytes 1179652
  112.1 2.2 %copy-start.10 = (bf16[512,384]{1,0:T(8,128)(2,1)S(1)}, bf16[512,384]{1,0:T(8,128)(2,1)}, u32[]{:S(2)}) copy-start(bf16[512,384]{1,0:T(8,128)(2,1)} %copy-done.9) | copy-start | bytes 1179652
